TPU v7x, 256 devices: a whole 4x4x8 slice. The times are simulated.
256 devices in a mesh: row: 2 (over core), col: 128 (over y, x, z).
Axes of the slice: x: 4, y: 4, z: 8, core: 2. Of those that a mesh axis runs over, the one named last changes fastest.
Arguments:
- observed: bfloat16 [1024, 16, 16384], P(None, 'row', 'col'), may hold values from -40 to 40
- library: bfloat16 [1024, 256], P('col'), may hold values from -0.1875 to 0.1875
Outputs:
- abundance: float32 [256, 16, 16384], P(None, 'row', 'col')
All inputs are finite; a program needn't handle non-finite values.
Results may differ from a plain program's by a relative error of at most 0.0024.
Values may be sent and summed in bfloat16 or wider, within the bound.
A program may use at most 128 MiB of HBM per device.

v0:
```python
import functools

import jax
import jax.numpy as jnp
from jax import lax
from jax.experimental import pallas as pl
from jax.experimental.pallas import tpu as pltpu
from jax.sharding import PartitionSpec as P

ITERS = 3
PROX = 8.0
WEIGHT_SPARSE = 0.3
WEIGHT_TV = 1.0
MESH = pl.DeviceIdType.MESH
F32 = jnp.float32
BF16 = jnp.bfloat16
VMEM = pl.BlockSpec(memory_space=pltpu.VMEM)


def depth_of(cols):
    return 8 if cols == 128 else 2


def slot_of(col, depth, cols):
    plane, z = col // depth, col % depth
    half = depth // 2
    return (z % 2) * (cols // 2) + plane * half + z // 2


def gather_kernel(cols, shard_ref, out_ref, packed, send_sem, recv_sem):
    depth = depth_of(cols)
    planes, half = cols // depth, depth // 2
    row, col = lax.axis_index("row"), lax.axis_index("col")
    plane, z = lax.div(col, depth), lax.rem(col, depth)
    parity = lax.rem(z, 2)

    def z_peer(step):
        return (row, plane * depth + lax.rem(z + step, depth))

    def plane_peer(step):
        return (row, lax.rem(plane + step, planes) * depth + z)

    core_peer = (1 - row, col)
    peers = [z_peer(s) for s in range(1, depth)] + [plane_peer(s) for s in range(1, planes)] + [core_peer]
    barrier = pltpu.get_barrier_semaphore()
    for peer in peers:
        pl.semaphore_signal(barrier, inc=1, device_id=peer, device_id_type=MESH)
    shard = shard_ref[...].astype(F32)
    packed[...] = jnp.concatenate([shard[:, :128], shard[:, 128:]], axis=0).astype(BF16)
    mine = parity * (cols // 2) + plane * half + lax.div(z, 2)
    pl.semaphore_wait(barrier, len(peers))

    @pl.when(row == parity)
    def _():
        out_ref[mine] = packed[...]
        for step in range(1, depth):
            pltpu.make_async_remote_copy(
                src_ref=packed,
                dst_ref=out_ref.at[mine],
                send_sem=send_sem.at[0],
                recv_sem=recv_sem.at[0],
                device_id=z_peer(step),
                device_id_type=MESH,
            ).start()
        if half > 1:
            got = out_ref.at[pl.ds(0, half - 1)]
            pltpu.make_async_copy(got, got, recv_sem.at[0]).wait()

    @pl.when(row != parity)
    def _():
        got = out_ref.at[pl.ds(0, half)]
        pltpu.make_async_copy(got, got, recv_sem.at[0]).wait()

    block = out_ref.at[pl.ds(row * (cols // 2) + plane * half, half)]
    for step in range(1, planes):
        pltpu.make_async_remote_copy(
            src_ref=block,
            dst_ref=block,
            send_sem=send_sem.at[1],
            recv_sem=recv_sem.at[1],
            device_id=plane_peer(step),
            device_id_type=MESH,
        ).start()
    got = out_ref.at[pl.ds(0, half * (planes - 1))]
    pltpu.make_async_copy(got, got, recv_sem.at[1]).wait()
    own_half = out_ref.at[pl.ds(row * (cols // 2), cols // 2)]
    swap = pltpu.make_async_remote_copy(
        src_ref=own_half,
        dst_ref=own_half,
        send_sem=send_sem.at[2],
        recv_sem=recv_sem.at[2],
        device_id=core_peer,
        device_id_type=MESH,
    )
    swap.start()

    @pl.when(row == parity)
    def _():
        sent = out_ref.at[pl.ds(0, depth - 1)]
        pltpu.make_async_copy(sent, sent, send_sem.at[0]).wait()

    pltpu.make_async_copy(got, got, send_sem.at[1]).wait()
    swap.wait()


def gather_library(library, cols):
    return pl.pallas_call(
        functools.partial(gather_kernel, cols),
        out_shape=jax.ShapeDtypeStruct((cols, 16, 128), BF16),
        in_specs=[VMEM],
        out_specs=VMEM,
        scratch_shapes=[
            pltpu.VMEM((16, 128), BF16),
            pltpu.SemaphoreType.DMA((3,)),
            pltpu.SemaphoreType.DMA((3,)),
        ],
        compiler_params=pltpu.CompilerParams(collective_id=0, has_side_effects=True),
        name="gather_library",
    )(library)


def small_inverse(m):
    def inv2(q):
        (a, b), (c, d) = q
        scale = 1.0 / (a * d - b * c)
        return [[d * scale, -b * scale], [-c * scale, a * scale]]

    def mul(x, y):
        return [[x[i][0] * y[0][j] + x[i][1] * y[1][j] for j in range(2)] for i in range(2)]

    def sub(x, y):
        return [[x[i][j] - y[i][j] for j in range(2)] for i in range(2)]

    a = [r[:2] for r in m[:2]]
    b = [r[2:] for r in m[:2]]
    c = [r[:2] for r in m[2:]]
    d = [r[2:] for r in m[2:]]
    ai = inv2(a)
    cai = mul(c, ai)
    aib = mul(ai, b)
    si = inv2(sub(d, mul(cai, b)))
    right = mul(aib, si)
    low = mul(si, cai)
    top = [[ai[i][j] + (right[i][0] * cai[0][j] + right[i][1] * cai[1][j]) for j in range(2)] for i in range(2)]
    return [
        top[0] + [-v for v in right[0]],
        top[1] + [-v for v in right[1]],
        [-v for v in low[0]] + si[0],
        [-v for v in low[1]] + si[1],
    ]


def eliminate(matrix):
    size, step = 128, 4
    groups = [matrix[8 * g : 8 * g + 8, :] for g in range(size // 8)]
    lane = lax.broadcasted_iota(jnp.int32, (8, size), 1)
    place = lax.broadcasted_iota(jnp.int32, (8, size), 0)
    full = (8, size)
    for first in range(0, size, step):
        home, shift = first // 8, first % 8
        cols = [
            [jnp.broadcast_to(g[:, first + a : first + a + 1], full) for a in range(step)] for g in groups
        ]
        pivot = [
            [jnp.broadcast_to(cols[home][b][shift + a : shift + a + 1, :], full) for b in range(step)]
            for a in range(step)
        ]
        turned = small_inverse(pivot)
        inside = (lane >= first) & (lane < first + step)
        rows = []
        for a in range(step):
            line = jnp.broadcast_to(groups[home][shift + a : shift + a + 1, :], full)
            line = jnp.where(inside, 0.0, line)
            rows.append(jnp.where(lane == first + a, 1.0, line))
        fresh = []
        for a in range(step):
            total = turned[a][0] * rows[0] + turned[a][1] * rows[1]
            fresh.append(total + (turned[a][2] * rows[2] + turned[a][3] * rows[3]))
        nxt = []
        for g, group in enumerate(groups):
            c = cols[g]
            kept = jnp.where(inside, 0.0, group)
            value = kept - (c[0] * fresh[0] + c[1] * fresh[1]) - (c[2] * fresh[2] + c[3] * fresh[3])
            if g == home:
                for a in range(step):
                    value = jnp.where(place == shift + a, fresh[a], value)
            nxt.append(value)
        groups = nxt
    return jnp.concatenate(groups, axis=0)


def exact_dot(a, b, dims):
    return lax.dot_general(a, b, (dims, ((), ())), precision=lax.Precision.HIGHEST, preferred_element_type=F32)


def split2(x):
    high = x.astype(BF16)
    return high, (x - high.astype(F32)).astype(BF16)


def setup_kernel(cols, obs_ref, lib_ref, inv_ref, gram_ref, proj_ref, square_ref, lib, wide):
    depth = depth_of(cols)
    channels = 8 * cols
    for pair in range(cols // 2):
        one = lib_ref[slot_of(2 * pair, depth, cols)].astype(F32)
        two = lib_ref[slot_of(2 * pair + 1, depth, cols)].astype(F32)
        lib[16 * pair : 16 * pair + 16, 0:128] = jnp.concatenate([one[0:8], two[0:8]], axis=0).astype(BF16)
        lib[16 * pair : 16 * pair + 16, 128:256] = jnp.concatenate([one[8:16], two[8:16]], axis=0).astype(BF16)
    library = lib[...]
    gram = lax.dot_general(library, library, (((0,), (0,)), ((), ())), preferred_element_type=F32)
    high, low = split2(gram)
    gram_ref[0:256, :] = high
    gram_ref[256:512, :] = low
    same = lax.broadcasted_iota(jnp.int32, (256, 256), 0) == lax.broadcasted_iota(jnp.int32, (256, 256), 1)
    system = gram + jnp.where(same, 1.0 + PROX, 0.0)

    a11, a12 = system[:128, :128], system[:128, 128:]
    a21, a22 = system[128:, :128], system[128:, 128:]
    x = eliminate(a11)
    y = exact_dot(x, a12, ((1,), (0,)))
    z = eliminate(a22 - exact_dot(a21, y, ((1,), (0,))))
    b12 = -exact_dot(y, z, ((1,), (0,)))
    b11 = x - exact_dot(b12, y, ((1,), (1,)))
    b21 = -exact_dot(z, y, ((1,), (1,)))
    inv_ref[0:128, 0:128] = b11
    inv_ref[0:128, 128:256] = b12
    inv_ref[128:256, 0:128] = b21
    inv_ref[128:256, 128:256] = z

    def widen(k, total):
        base = pl.multiple_of(k * 16, 16)
        part = obs_ref[pl.ds(base, 16)].astype(F32)
        wide[pl.ds(pl.multiple_of(base * 8, 128), 128), :] = part.reshape(128, 128)
        return total + jnp.sum(part * part, axis=0)

    square_ref[...] = lax.fori_loop(0, channels // 16, widen, jnp.zeros((8, 128), F32))
    flip = lax.axis_index("row") == 1

    def project(i, carry):
        source = jnp.where(flip, 7 - i, i)
        part = wide[pl.ds(source, channels, stride=8), :].astype(BF16)
        proj_ref[pl.ds(pl.multiple_of(i * 128, 128), 128), :] = lax.dot_general(
            part, lib[...], (((0,), (0,)), ((), ())), preferred_element_type=F32
        )
        return carry

    lax.fori_loop(0, 8, project, 0)


def set_up(observed, gathered, cols):
    channels = 8 * cols
    return pl.pallas_call(
        functools.partial(setup_kernel, cols),
        out_shape=[
            jax.ShapeDtypeStruct((256, 256), F32),
            jax.ShapeDtypeStruct((512, 256), BF16),
            jax.ShapeDtypeStruct((1024, 256), F32),
            jax.ShapeDtypeStruct((8, 128), F32),
        ],
        in_specs=[VMEM, VMEM],
        out_specs=[VMEM] * 4,
        scratch_shapes=[pltpu.VMEM((channels, 256), BF16), pltpu.VMEM((channels * 8, 128), F32)],
        compiler_params=pltpu.CompilerParams(vmem_limit_bytes=24 * 2**20),
        name="set_up",
    )(observed, gathered)


CHUNK = 32
PAD = 136


def fold(x):
    total = None
    for k in range(x.shape[0] // 8):
        for half in range(2):
            part = x[8 * k : 8 * k + 8, 128 * half : 128 * half + 128]
            total = part if total is None else total + part
    return total


def iterate_kernel(
    cols,
    inv_ref,
    gram_ref,
    proj_ref,
    square_ref,
    out_ref,
    est,
    part_a,
    part_b,
    rim_send,
    rim_left,
    rim_right,
    halo,
    ghost,
    sparse_var,
    sparse_dual,
    down_var,
    down_dual,
    down_arg,
    right_var,
    right_dual,
    right_arg,
    mix,
    gram_mix,
    inv3,
    sums,
    near,
    far,
    halo_sem,
    rim_sem,
    sum_sem,
):
    depth = depth_of(cols)
    planes = cols // depth
    row, col = lax.axis_index("row"), lax.axis_index("col")
    plane, z = lax.div(col, depth), lax.rem(col, depth)
    core_peer = (1 - row, col)
    left = (row, lax.rem(col + cols - 1, cols))
    right = (row, lax.rem(col + 1, cols))
    here = z * 2 + row
    pack = 2 * depth

    def near_peer(step):
        other = lax.rem(here + step, pack)
        return (lax.rem(other, 2), plane * depth + lax.div(other, 2))

    def far_peer(step):
        return (row, lax.rem(plane + step, planes) * depth + z)

    peers = (
        [near_peer(s) for s in range(1, pack)] + [far_peer(s) for s in range(1, planes)] + [left, right, core_peer]
    )
    barrier = pltpu.get_barrier_semaphore()
    for peer in peers:
        pl.semaphore_signal(barrier, inc=1, device_id=peer, device_id_type=MESH)

    high, low = split2(inv_ref[...])
    inv3[0:256, :] = high
    inv3[256:512, :] = low
    inv3[512:768, :] = high

    def rows_of(x):
        return pl.ds(pl.multiple_of(x * 128, 128), 128)

    def stacked(x):
        one, two = split2(x)
        return jnp.concatenate([one, one, two], axis=1)

    def solve(x):
        return jnp.dot(stacked(x), inv3[...], preferred_element_type=F32)

    def solve_turned(x):
        one, two = split2(x)
        dims = (((1,), (1,)), ((), ()))
        total = lax.dot_general(inv3[0:256, :], one, dims, preferred_element_type=F32)
        total = total + lax.dot_general(inv3[256:512, :], one, dims, preferred_element_type=F32)
        return total + lax.dot_general(inv3[0:256, :], two, dims, preferred_element_type=F32)

    def send_halo(turn, slot, field):
        copy = pltpu.make_async_remote_copy(
            src_ref=field.at[rows_of(7)],
            dst_ref=halo.at[turn, slot],
            send_sem=halo_sem.at[0, turn, slot],
            recv_sem=halo_sem.at[1, turn, slot],
            device_id=core_peer,
            device_id_type=MESH,
        )
        copy.start()
        return copy

    def send_rims(turn):
        used = 8 if turn == 0 else 16
        to_left = pltpu.make_async_remote_copy(
            src_ref=rim_send.at[turn, 0, pl.ds(0, used)],
            dst_ref=rim_right.at[turn, pl.ds(0, used)],
            send_sem=rim_sem.at[0, turn, 0],
            recv_sem=rim_sem.at[1, turn, 0],
            device_id=left,
            device_id_type=MESH,
        )
        to_right = pltpu.make_async_remote_copy(
            src_ref=rim_send.at[turn, 1, pl.ds(0, used)],
            dst_ref=rim_left.at[turn, pl.ds(0, used)],
            send_sem=rim_sem.at[0, turn, 1],
            recv_sem=rim_sem.at[1, turn, 1],
            device_id=right,
            device_id_type=MESH,
        )
        to_left.start()
        to_right.start()
        return [to_left, to_right]

    def put_rims(turn, i, slot, value):
        rim_send[turn, 0, pl.ds(8 * slot + i, 1), :] = value[0:1, :]
        rim_send[turn, 1, pl.ds(8 * slot + i, 1), :] = value[127:128, :]

    for i in range(8):
        value = solve(proj_ref[128 * i : 128 * i + 128, :])
        part_a[128 * i : 128 * i + 128, :] = value
        put_rims(0, i, 0, value)

    pl.semaphore_wait(barrier, len(peers))
    rim_copies = send_rims(0)
    halo_copies = [send_halo(0, 0, part_a)]

    def start_sums(turn, stage):
        buffer = (near, far)[stage]
        peer_of, count = ((near_peer, pack), (far_peer, planes))[stage]
        index = (here, plane)[stage]
        for step in range(1, count):
            pltpu.make_async_remote_copy(
                src_ref=sums.at[turn, stage],
                dst_ref=buffer.at[turn, pl.ds(index, 1)],
                send_sem=sum_sem.at[0, turn, stage],
                recv_sem=sum_sem.at[1, turn, stage],
                device_id=peer_of(step),
                device_id_type=MESH,
            ).start()

    def wait_sums(turn, stage, which):
        buffer = (near, far)[stage]
        count = (pack, planes)[stage]
        got = buffer.at[turn, pl.ds(0, count - 1)]
        pltpu.make_async_copy(got, got, sum_sem.at[which, turn, stage]).wait()

    first_col = jnp.where(col == 0, 1.0, 0.0).astype(F32)
    last_col = jnp.where(col == cols - 1, 1.0, 0.0).astype(F32)
    lanes = lax.broadcasted_iota(jnp.int32, (1, 128), 1)
    penalty, rescale, carry_c, carry_s = 1.0, 0.0, 0.0, 0.0

    def scalar(x):
        return x if isinstance(x, float) else x[0, 0]

    for turn in range(ITERS):
        start = turn == 0
        old_c, old_s = carry_c, carry_s
        pc_v = penalty * old_c
        sigma_v = 1.0 - pc_v * old_s
        share_v = 1.0 / (1.0 + penalty)
        carry_s = 1.0 + old_c * old_s
        bound, cut = scalar(WEIGHT_TV / penalty), scalar(WEIGHT_SPARSE / penalty)
        pc, sigma, scale_c = scalar(pc_v), scalar(sigma_v), scalar(old_c)
        share, ratio, scale_s = scalar(share_v), scalar(penalty * share_v), scalar(carry_s)
        factor = scalar(rescale)
        for copy in rim_copies + halo_copies:
            copy.wait()

        def combined(a, b):
            return a if start else a + factor * b

        def place(i, carry):
            value = combined(part_a[rows_of(i), :], part_b[rows_of(i), :])
            est[i, 0:128, :] = value
            return carry

        lax.fori_loop(0, 8, place, 0)
        est[8, 0:128, :] = combined(halo[turn, 0], halo[turn, 1])
        own_first = combined(rim_send[turn, 0, 0:8, :], rim_send[turn, 0, 8:16, :])
        own_last = combined(rim_send[turn, 1, 0:8, :], rim_send[turn, 1, 8:16, :])
        from_right = combined(rim_right[turn, 0:8, :], rim_right[turn, 8:16, :])
        from_left = combined(rim_left[turn, 0:8, :], rim_left[turn, 8:16, :])
        from_right = jnp.where(last_col > 0.0, own_last, from_right)
        from_left = jnp.where(first_col > 0.0, own_first, from_left)
        for i in range(8):
            est[i, 128:129, :] = from_right[i : i + 1, :]

        g_diff = own_first - from_left
        g_sum = g_diff if start else g_diff + factor * ghost[...]
        g_dual = jnp.clip(g_sum, -bound, bound)
        g_arg = g_diff - (g_sum - g_dual)
        ghost[...] = g_dual
        for i in range(8):
            right_arg[i, 7:8, :] = g_arg[i : i + 1, :]
            right_dual[i, 7:8, :] = g_dual[i : i + 1, :]

        def update(i, off, totals):
            at = pl.ds(off, CHUNK)
            shifted = pl.ds(off + 8, CHUNK)
            flat = pl.ds(pl.multiple_of(i * 128 + off, CHUNK), CHUNK)
            primal, dual, data = totals
            e = est[i, at, :]
            half = e.astype(BF16)
            gh = jnp.dot(jnp.concatenate([half, half], axis=1), gram_ref[...], preferred_element_type=F32)
            h = half.astype(F32)
            w = proj_ref[flat, :]
            if start:
                data = data + fold(h * (gh - 2.0 * w))
                mix[flat, :] = h
                gram_mix[flat, :] = gh
            else:
                y, gy = mix[flat, :], gram_mix[flat, :]
                data = data + fold((h - pc * y) * (gh - pc * gy - (2.0 * sigma) * w))
                mix[flat, :] = h + scale_c * y
                gram_mix[flat, :] = gh + scale_c * gy
            t = e if start else e + factor * sparse_dual[flat, :]
            fresh = jnp.maximum(t - cut, 0.0)
            gap = e - fresh
            primal = primal + fold(gap * gap)
            move = fresh if start else fresh - sparse_var[flat, :]
            dual = dual + fold(move * move)
            sparse_var[flat, :] = fresh
            sparse_dual[flat, :] = t - fresh
            d = est[i + 1, at, :] - e
            t = d if start else d + factor * down_dual[flat, :]
            clipped = jnp.clip(t, -bound, bound)
            fresh = t - clipped
            gap = d - fresh
            move = fresh if start else fresh - down_var[flat, :]
            weight = jnp.where((i == 7) & (row == 1), 0.0, 1.0).astype(F32)
            primal = primal + weight * fold(gap * gap)
            dual = dual + weight * fold(move * move)
            down_var[flat, :] = fresh
            down_dual[flat, :] = clipped
            down_arg[flat, :] = gap
            d = est[i, pl.ds(off + 1, CHUNK), :] - e
            t = d if start else d + factor * right_dual[i, shifted, :]
            clipped = jnp.clip(t, -bound, bound)
            fresh = t - clipped
            gap = d - fresh
            primal = primal + fold(gap * gap)
            move = fresh if start else fresh - right_var[flat, :]
            dual = dual + fold(move * move)
            right_var[flat, :] = fresh
            right_dual[i, shifted, :] = clipped
            right_arg[i, shifted, :] = gap
            return primal, dual, data

        def update_row(i, totals):
            for off in range(0, 128, CHUNK):
                totals = update(i, off, totals)
            return totals

        zero = jnp.zeros((8, 128), F32)
        primal, dual, data = lax.fori_loop(0, 8, update_row, (zero, zero, zero))
        data = (data + (sigma * sigma) * square_ref[...]) * (share * share)
        line_p = jnp.sum(primal + data, axis=0, keepdims=True)
        line_d = jnp.sum(dual, axis=0, keepdims=True)
        line_p = line_p + pltpu.roll(line_p, 64, 1)
        line_d = line_d + pltpu.roll(line_d, 64, 1)
        line = jnp.where(lanes < 64, line_p, line_d)
        sums[turn, 0] = line
        near[turn, pl.ds(here, 1), :] = line
        start_sums(turn, 0)

        final = turn == ITERS - 1

        def rhs(i):
            flat = rows_of(i)
            above = rows_of(jnp.maximum(i - 1, 0))
            has_above = jnp.where(i > 0, 1.0, 0.0).astype(F32)
            w = proj_ref[flat, :]
            we = gram_mix[flat, :] - scale_s * w
            at = pl.ds(8, 128)
            before = pl.ds(7, 128)
            adj_a = (has_above * down_arg[above, :] - down_arg[flat, :]) + (
                right_arg[i, before, :] - right_arg[i, at, :]
            )
            adj_b = (has_above * down_dual[above, :] - down_dual[flat, :]) + (
                right_dual[i, before, :] - right_dual[i, at, :]
            )
            a = w + ratio * we + sparse_var[flat, :] + PROX * est[i, 0:128, :] - adj_a
            b = -(share * we + sparse_dual[flat, :] + adj_b)
            return a, b

        def prepare(i, carry):
            a, b = rhs(i)
            a, b = solve(a), solve(b)
            part_a[rows_of(i), :] = a
            part_b[rows_of(i), :] = b
            put_rims(turn + 1, i, 0, a)
            put_rims(turn + 1, i, 1, b)
            return carry

        def prepare_final(i, carry):
            a, b = rhs(i)
            out_ref[jnp.where(row == 1, 7 - i, i)] = solve_turned(a)
            turned = solve_turned(b)
            part_b[rows_of(i), 0:128] = turned[0:128, :]
            part_b[rows_of(i), 128:256] = turned[128:256, :]
            return carry

        work = prepare_final if final else prepare
        lax.fori_loop(0, 4, work, 0)
        wait_sums(turn, 0, 1)
        line = jnp.sum(near[turn], axis=0, keepdims=True)
        sums[turn, 1] = line
        far[turn, pl.ds(plane, 1), :] = line
        start_sums(turn, 1)
        lax.fori_loop(4, 8, work, 0)
        if not final:
            rim_copies = send_rims(turn + 1)
            halo_copies = [send_halo(turn + 1, 0, part_a), send_halo(turn + 1, 1, part_b)]
        wait_sums(turn, 1, 1)
        line = jnp.sum(far[turn], axis=0, keepdims=True)
        total_p = jnp.sum(jnp.where(lanes < 64, line, 0.0), axis=1, keepdims=True)
        total_d = jnp.sum(jnp.where(lanes < 64, 0.0, line), axis=1, keepdims=True)
        root = jnp.sqrt(jnp.sqrt((total_p + 1.0) / (penalty * penalty * total_d + 1.0)))
        following = penalty * root
        rescale = penalty / following
        carry_c = rescale * share_v
        penalty = following

    factor = scalar(rescale)

    def finish(i, carry):
        at = jnp.where(row == 1, 7 - i, i)
        out_ref[at, 0:128, :] = out_ref[at, 0:128, :] + factor * part_b[rows_of(i), 0:128]
        out_ref[at, 128:256, :] = out_ref[at, 128:256, :] + factor * part_b[rows_of(i), 128:256]
        return carry

    lax.fori_loop(0, 8, finish, 0)
    for turn in range(ITERS):
        for stage in range(2):
            wait_sums(turn, stage, 0)


def iterate(inverse, gram, proj, square, cols):
    depth = depth_of(cols)
    field = pltpu.VMEM((1024, 256), F32)
    padded = pltpu.VMEM((8, PAD, 256), F32)
    rims = pltpu.VMEM((ITERS, 16, 256), F32)
    return pl.pallas_call(
        functools.partial(iterate_kernel, cols),
        out_shape=jax.ShapeDtypeStruct((8, 256, 128), F32),
        in_specs=[VMEM] * 4,
        out_specs=VMEM,
        scratch_shapes=[
            pltpu.VMEM((9, PAD, 256), F32),
            field,
            field,
            pltpu.VMEM((ITERS, 2, 16, 256), F32),
            rims,
            rims,
            pltpu.VMEM((ITERS, 2, 128, 256), F32),
            pltpu.VMEM((8, 256), F32),
            field,
            field,
            field,
            field,
            field,
            field,
            padded,
            padded,
            field,
            field,
            pltpu.VMEM((768, 256), BF16),
            pltpu.VMEM((ITERS, 2, 1, 128), F32),
            pltpu.VMEM((ITERS, 2 * depth, 128), F32),
            pltpu.VMEM((ITERS, cols // depth, 128), F32),
            pltpu.SemaphoreType.DMA((2, ITERS, 2)),
            pltpu.SemaphoreType.DMA((2, ITERS, 2)),
            pltpu.SemaphoreType.DMA((2, ITERS, 2)),
        ],
        compiler_params=pltpu.CompilerParams(
            collective_id=1, has_side_effects=True, vmem_limit_bytes=32 * 2**20
        ),
        name="iterate",
    )(inverse, gram, proj, square)


def on_device(cols, observed, library):
    gathered = gather_library(library, cols)
    inverse, gram, proj, square = set_up(observed, gathered, cols)
    return iterate(inverse, gram, proj, square, cols).transpose(1, 0, 2)


def solution(mesh):
    return jax.shard_map(
        functools.partial(on_device, mesh.shape["col"]),
        mesh=mesh,
        in_specs=(P(None, "row", "col"), P("col", None)),
        out_specs=P(None, "row", "col"),
        check_vma=False,
    )
```

profile of v0, /device:TPU:1, one launch (start us, length us, event | category | flops | bytes accessed | tf_op | source)
XLA Modules:
  0.0 95.1 jit_solution(12381513738712553123)
XLA Ops:
  0.0 22.9 %gather_library.1.lib_ref = bf16[128,16,128]{2,1,0:T(8,128)(2,1)} custom-call(bf16[8,256]{1,0:T(8,128)(2,1)} %shard_ref.1), custom_call_target="tpu_custom_call" | custom-call | tf_op jit(solution)/shard_map/gather_library/pallas_call | solution.py:107
  22.9 0.0 copy-start
  22.9 1.6 %copy-done = bf16[1024,8,128]{2,1,0:T(8,128)(2,1)S(1)} copy-done((bf16[1024,8,128]{2,1,0:T(8,128)(2,1)S(1)}, bf16[1024,8,128]{2,1,0:T(8,128)(2,1)}, u32[]{:S(2)}) %copy-start) | copy-done | bytes 2097176
  24.5 0.0 copy-start.1
  24.5 1.0 %copy-done.1 = bf16[128,16,128]{2,1,0:T(8,128)(2,1)S(1)} copy-done((bf16[128,16,128]{2,1,0:T(8,128)(2,1)S(1)}, bf16[128,16,128]{2,1,0:T(8,128)(2,1)}, u32[]{:S(2)}) %copy-start.1) | copy-done | bytes 524312
  25.5 22.0 %set_up.1 = (f32[256,256]{1,0:T(8,128)S(1)}, bf16[512,256]{1,0:T(8,128)(2,1)S(1)}, f32[1024,256]{1,0:T(8,128)S(1)}, f32[8,128]{1,0:T(8,128)S(1)}) custom-call(bf16[1024,8,128]{2,1,0:T(8,128)(2,1)S(1)} %copy-done, bf16[128,16,128]{2,1,0:T(8,128)(2,1)S(1)} %copy-done.1), custom_call_target="tpu_custom_call" | custom-call | tf_op jit(solution)/shard_map/set_up/pallas_call | solution.py:252
  47.6 46.0 %iterate.1 = f32[8,256,128]{2,1,0:T(8,128)S(1)} custom-call(f32[256,256]{1,0:T(8,128)S(1)} %get-tuple-element.9.inv_ref, bf16[512,256]{1,0:T(8,128)(2,1)S(1)} %get-tuple-element.10.gram_ref, f32[1024,256]{1,0:T(8,128)S(1)} %get-tuple-element.11.proj_ref, f32[8,128]{1,0:T(8,128)S(1)} %get-tuple-element.12.square_ref), custom_call_target="tpu_custom_call" | custom-call | tf_op jit(solution)/shard_map/iterate/pallas_call | solution.py:623
  93.6 1.6 %copy.3 = f32[256,8,128]{2,1,0:T(8,128)} copy(f32[256,8,128]{2,0,1:T(8,128)S(1)} %bitcast.1) | data formatting | bytes 2097152 | tf_op jit(solution)/shard_map/transpose | solution.py:665
Async XLA Ops:
  22.9 1.6 %copy-start = (bf16[1024,8,128]{2,1,0:T(8,128)(2,1)S(1)}, bf16[1024,8,128]{2,1,0:T(8,128)(2,1)}, u32[]{:S(2)}) copy-start(bf16[1024,8,128]{2,1,0:T(8,128)(2,1)} %obs_ref.1) | copy-start | bytes 6291460
  24.5 1.0 %copy-start.1 = (bf16[128,16,128]{2,1,0:T(8,128)(2,1)S(1)}, bf16[128,16,128]{2,1,0:T(8,128)(2,1)}, u32[]{:S(2)}) copy-start(bf16[128,16,128]{2,1,0:T(8,128)(2,1)} %gather_library.1.lib_ref) | copy-start | bytes 1572868
where the time goes:
time: 95.3 us; the launch traced here: 95.1 us
  Pallas kernels  90.9 us (95%)
  local copies, waits for them, and re-layouts  4.21 us (4%)
    pallas_call x1, Pallas kernels, iterate(): pl.pallas_call(functools.partial(iterate_kernel, cols), out_shape=jax.Sha...  46 us
    pallas_call x1, Pallas kernels, gather_library(): pl.pallas_call(functools.partial(gather_kernel, cols), out_shape=jax.Shap...  22.9 us
    pallas_call x1, Pallas kernels, set_up(): pl.pallas_call(functools.partial(setup_kernel, cols), out_shape=[jax.Shap...  22 us
    unnamed x4, local copies, waits for them, and re-layouts  2.63 us

commit v1 on v0

v1 whole, which is shorter than its diff:
```python
import functools

import jax
import jax.numpy as jnp
from jax import lax
from jax.experimental import pallas as pl
from jax.experimental.pallas import tpu as pltpu
from jax.sharding import PartitionSpec as P

ITERS = 3
PROX = 8.0
WEIGHT_SPARSE = 0.3
WEIGHT_TV = 1.0
MESH = pl.DeviceIdType.MESH
F32 = jnp.float32
BF16 = jnp.bfloat16
VMEM = pl.BlockSpec(memory_space=pltpu.VMEM)


def slot_of(col, depth, cols):
    plane, z = col // depth, col % depth
    half = depth // 2
    return (z % 2) * (cols // 2) + plane * half + z // 2


def dot_of(x, y):
    t = [a * b for a, b in zip(x, y)]
    while len(t) > 1:
        t = [t[i] + t[i + 1] if i + 1 < len(t) else t[i] for i in range(0, len(t), 2)]
    return t[0]

def symmetric_inverse(m):
    n = len(m)
    if n == 1:
        return [[1.0 / m[0][0]]]
    if n == 2:
        scale = 1.0 / (m[0][0] * m[1][1] - m[0][1] * m[0][1])
        off = -m[0][1] * scale
        return [[m[1][1] * scale, off], [off, m[0][0] * scale]]
    h = n // 2
    a = symmetric_inverse([r[:h] for r in m[:h]])
    b = [r[h:] for r in m[:h]]
    bt = [list(c) for c in zip(*b)]
    t = [[dot_of(a[i], bt[j]) for j in range(h)] for i in range(h)]
    tt = [list(c) for c in zip(*t)]
    s = [[None] * h for _ in range(h)]
    for i in range(h):
        for j in range(i, h):
            s[i][j] = s[j][i] = m[h + i][h + j] - dot_of(bt[i], tt[j])
    s = symmetric_inverse(s)
    u = [[dot_of(t[i], s[j]) for j in range(h)] for i in range(h)]
    top = [[None] * h for _ in range(h)]
    for i in range(h):
        for j in range(i, h):
            top[i][j] = top[j][i] = a[i][j] + dot_of(u[i], t[j])
    out = [[None] * n for _ in range(n)]
    for i in range(h):
        for j in range(h):
            out[i][j] = top[i][j]
            out[h + i][h + j] = s[i][j]
            out[i][h + j] = -u[i][j]
            out[h + j][i] = -u[i][j]
    return out

def eliminate(matrix, ref):
    size, step = 128, 8
    groups = [matrix[8 * g : 8 * g + 8, :] for g in range(size // 8)]
    lane = lax.broadcasted_iota(jnp.int32, (8, size), 1)
    place = lax.broadcasted_iota(jnp.int32, (8, size), 0)
    full = (8, size)
    for home, first in enumerate(range(0, size, step)):

        def cols_of(g):
            return [jnp.broadcast_to(g[:, first + a : first + a + 1], full) for a in range(step)]

        home_cols = cols_of(groups[home])
        ref[0:8, :] = groups[home]
        for b in range(step):
            ref[8 + 8 * b : 16 + 8 * b, :] = home_cols[b]
        line = [jnp.broadcast_to(ref[a : a + 1, :], full) for a in range(step)]
        pivot = [[None] * step for _ in range(step)]
        for a in range(step):
            for b in range(a, step):
                spot = 8 + 8 * b + a
                pivot[a][b] = pivot[b][a] = jnp.broadcast_to(ref[spot : spot + 1, :], full)
        turned = symmetric_inverse(pivot)
        inside = (lane >= first) & (lane < first + step)
        rows = [jnp.where(lane == first + a, 1.0, jnp.where(inside, 0.0, line[a])) for a in range(step)]
        fresh = [dot_of(turned[a], rows) for a in range(step)]
        nxt = []
        for g, group in enumerate(groups):
            if g == home:
                value = fresh[0]
                for a in range(1, step):
                    value = jnp.where(place == a, fresh[a], value)
            else:
                value = jnp.where(inside, 0.0, group) - dot_of(cols_of(group), fresh)
            nxt.append(value)
        groups = nxt
    return jnp.concatenate(groups, axis=0)


def exact_dot(a, b, dims):
    return lax.dot_general(a, b, (dims, ((), ())), precision=lax.Precision.HIGHEST, preferred_element_type=F32)


def split2(x):
    high = x.astype(BF16)
    return high, (x - high.astype(F32)).astype(BF16)


CHUNK = 32
PAD = 136


def fold(x):
    total = None
    for k in range(x.shape[0] // 8):
        for half in range(2):
            part = x[8 * k : 8 * k + 8, 128 * half : 128 * half + 128]
            total = part if total is None else total + part
    return total


def kernel(
    sizes,
    obs_ref,
    shard_ref,
    out_ref,
    obs,
    wide,
    turned_obs,
    packed,
    shards,
    lib,
    work_rows,
    inverse,
    gram2,
    inv3,
    proj,
    own_rims,
    est,
    part_a,
    part_b,
    rim_send,
    rim_left,
    rim_right,
    halo,
    ghost,
    sparse_var,
    sparse_dual,
    down_var,
    down_dual,
    down_arg,
    right_var,
    right_dual,
    right_arg,
    mix,
    gram_mix,
    sums,
    pair,
    far,
    obs_sem,
    gather_sem,
    halo_sem,
    rim_sem,
    sum_sem,
):
    ys, xs, depth = sizes
    planes, half = ys * xs, depth // 2
    cols = planes * depth
    channels = 8 * cols
    row, col = lax.axis_index("row"), lax.axis_index("col")
    plane, z = lax.div(col, depth), lax.rem(col, depth)
    y, x = lax.div(plane, xs), lax.rem(plane, xs)
    parity = lax.rem(z, 2)
    flip = row == 1
    core_peer = (1 - row, col)
    left = (row, lax.rem(col + cols - 1, cols))
    right = (row, lax.rem(col + 1, cols))

    def peer_at(dy, dx, dz):
        return (row, (lax.rem(y + dy, ys) * xs + lax.rem(x + dx, xs)) * depth + lax.rem(z + dz, depth))

    def z_peer(step):
        return peer_at(0, 0, step)

    def plane_peer(step):
        return peer_at(step // xs, step % xs, 0)

    obs_copy = pltpu.make_async_copy(obs_ref, obs, obs_sem)
    obs_copy.start()
    barrier = pltpu.get_barrier_semaphore()
    for dz in range(depth):
        for dy in range(ys):
            for dx in range(xs):
                if dy or dx or dz:
                    pl.semaphore_signal(barrier, inc=1, device_id=peer_at(dy, dx, dz), device_id_type=MESH)
    pl.semaphore_signal(barrier, inc=1, device_id=core_peer, device_id_type=MESH)
    shard = shard_ref[...].astype(F32)
    packed[...] = jnp.concatenate([shard[:, :128], shard[:, 128:]], axis=0).astype(BF16)
    mine = parity * (cols // 2) + plane * half + lax.div(z, 2)
    obs_copy.wait()

    def widen(k, total):
        base = pl.multiple_of(k * 16, 16)
        part = obs[pl.ds(base, 16)].astype(F32)
        wide[pl.ds(pl.multiple_of(base * 8, 128), 128), :] = part.reshape(128, 128)
        return total + jnp.sum(part * part, axis=0)

    square = lax.fori_loop(0, channels // 16, widen, jnp.zeros((8, 128), F32))
    pl.semaphore_wait(barrier, cols)

    @pl.when(row == parity)
    def _():
        for step in range(1, depth):
            pltpu.make_async_remote_copy(
                src_ref=packed,
                dst_ref=shards.at[mine],
                send_sem=gather_sem.at[0],
                recv_sem=gather_sem.at[1],
                device_id=z_peer(step),
                device_id_type=MESH,
            ).start()
        shards[mine] = packed[...]

    def turn_rows(i, carry):
        source = jnp.where(flip, 7 - i, i)
        part = wide[pl.ds(source, channels, stride=8), :]
        turned_obs[pl.ds(pl.multiple_of(i * 128, 128), 128), :] = part.T.astype(BF16)
        return carry

    lax.fori_loop(0, 4, turn_rows, 0)

    @pl.when(row == parity)
    def _():
        if half > 1:
            got = shards.at[pl.ds(0, half - 1)]
            pltpu.make_async_copy(got, got, gather_sem.at[1]).wait()

    @pl.when(row != parity)
    def _():
        got = shards.at[pl.ds(0, half)]
        pltpu.make_async_copy(got, got, gather_sem.at[1]).wait()

    block = shards.at[pl.ds(row * (cols // 2) + plane * half, half)]
    for step in range(1, planes):
        pltpu.make_async_remote_copy(
            src_ref=block,
            dst_ref=block,
            send_sem=gather_sem.at[2],
            recv_sem=gather_sem.at[3],
            device_id=plane_peer(step),
            device_id_type=MESH,
        ).start()
    lax.fori_loop(4, 8, turn_rows, 0)
    got = shards.at[pl.ds(0, half * (planes - 1))]
    pltpu.make_async_copy(got, got, gather_sem.at[3]).wait()
    own_half = shards.at[pl.ds(row * (cols // 2), cols // 2)]
    swap = pltpu.make_async_remote_copy(
        src_ref=own_half,
        dst_ref=own_half,
        send_sem=gather_sem.at[4],
        recv_sem=gather_sem.at[5],
        device_id=core_peer,
        device_id_type=MESH,
    )
    swap.start()

    @pl.when(row == parity)
    def _():
        sent = shards.at[pl.ds(0, depth - 1)]
        pltpu.make_async_copy(sent, sent, gather_sem.at[0]).wait()

    pltpu.make_async_copy(got, got, gather_sem.at[2]).wait()
    swap.wait()

    for two in range(cols // 2):
        one = shards[slot_of(2 * two, depth, cols)].astype(F32)
        other = shards[slot_of(2 * two + 1, depth, cols)].astype(F32)
        lib[16 * two : 16 * two + 16, 0:128] = jnp.concatenate([one[0:8], other[0:8]], axis=0).astype(BF16)
        lib[16 * two : 16 * two + 16, 128:256] = jnp.concatenate([one[8:16], other[8:16]], axis=0).astype(BF16)

    def rows_of(x):
        return pl.ds(pl.multiple_of(x * 128, 128), 128)

    for i in range(8):
        value = jnp.dot(turned_obs[128 * i : 128 * i + 128, :], lib[...], preferred_element_type=F32)
        proj[128 * i : 128 * i + 128, :] = value
        rim_send[0, 0, i : i + 1, :] = value[0:1, :]
        rim_send[0, 1, i : i + 1, :] = value[127:128, :]

    def send_halo(turn, slot, field):
        copy = pltpu.make_async_remote_copy(
            src_ref=field.at[rows_of(7)],
            dst_ref=halo.at[turn, slot],
            send_sem=halo_sem.at[0, turn, slot],
            recv_sem=halo_sem.at[1, turn, slot],
            device_id=core_peer,
            device_id_type=MESH,
        )
        copy.start()
        return copy

    def send_rims(turn):
        used = 8 if turn == 0 else 16
        to_left = pltpu.make_async_remote_copy(
            src_ref=rim_send.at[turn, 0, pl.ds(0, used)],
            dst_ref=rim_right.at[turn, pl.ds(0, used)],
            send_sem=rim_sem.at[0, turn, 0],
            recv_sem=rim_sem.at[1, turn, 0],
            device_id=left,
            device_id_type=MESH,
        )
        to_right = pltpu.make_async_remote_copy(
            src_ref=rim_send.at[turn, 1, pl.ds(0, used)],
            dst_ref=rim_left.at[turn, pl.ds(0, used)],
            send_sem=rim_sem.at[0, turn, 1],
            recv_sem=rim_sem.at[1, turn, 1],
            device_id=right,
            device_id_type=MESH,
        )
        to_left.start()
        to_right.start()
        return [to_left, to_right]

    rim_copies = send_rims(0)
    halo_copies = [send_halo(0, 0, proj)]

    library = lib[...]
    gram = lax.dot_general(library, library, (((0,), (0,)), ((), ())), preferred_element_type=F32)
    high, low = split2(gram)
    gram2[0:256, :] = high
    gram2[256:512, :] = low
    same = lax.broadcasted_iota(jnp.int32, (256, 256), 0) == lax.broadcasted_iota(jnp.int32, (256, 256), 1)
    system = gram + jnp.where(same, 1.0 + PROX, 0.0)
    first_inverse = eliminate(system[:128, :128], work_rows)
    lead = exact_dot(first_inverse, system[:128, 128:], ((1,), (0,)))
    last_inverse = eliminate(
        system[128:, 128:] - exact_dot(system[128:, :128], lead, ((1,), (0,))), work_rows
    )
    corner = -exact_dot(lead, last_inverse, ((1,), (0,)))
    inverse[0:128, 0:128] = first_inverse - exact_dot(corner, lead, ((1,), (1,)))
    inverse[0:128, 128:256] = corner
    inverse[128:256, 0:128] = -exact_dot(last_inverse, lead, ((1,), (1,)))
    inverse[128:256, 128:256] = last_inverse
    high, low = split2(inverse[...])
    inv3[0:256, :] = high
    inv3[256:512, :] = low
    inv3[512:768, :] = high

    def stacked(x):
        one, two = split2(x)
        return jnp.concatenate([one, one, two], axis=1)

    def solve(x):
        return jnp.dot(stacked(x), inv3[...], preferred_element_type=F32)

    def solve_turned(x):
        one, two = split2(x)
        dims = (((1,), (1,)), ((), ()))
        total = lax.dot_general(inv3[0:256, :], one, dims, preferred_element_type=F32)
        total = total + lax.dot_general(inv3[256:512, :], one, dims, preferred_element_type=F32)
        return total + lax.dot_general(inv3[0:256, :], two, dims, preferred_element_type=F32)

    def put_rims(turn, i, slot, value):
        rim_send[turn, 0, pl.ds(8 * slot + i, 1), :] = value[0:1, :]
        rim_send[turn, 1, pl.ds(8 * slot + i, 1), :] = value[127:128, :]

    for i in range(8):
        value = solve(proj[128 * i : 128 * i + 128, :])
        part_a[128 * i : 128 * i + 128, :] = value
        own_rims[0, i : i + 1, :] = value[0:1, :]
        own_rims[1, i : i + 1, :] = value[127:128, :]

    def send_pair(turn):
        pltpu.make_async_remote_copy(
            src_ref=sums.at[turn, 0],
            dst_ref=pair.at[turn],
            send_sem=sum_sem.at[0, turn, 0],
            recv_sem=sum_sem.at[1, turn, 0],
            device_id=core_peer,
            device_id_type=MESH,
        ).start()

    def send_sums(turn, dz, alone):
        for dy in range(ys):
            for dx in range(xs):
                copy = pltpu.make_async_remote_copy(
                    src_ref=sums.at[turn, 1],
                    dst_ref=far.at[turn, pl.ds(col, 1)],
                    send_sem=sum_sem.at[0, turn, 1],
                    recv_sem=sum_sem.at[1, turn, 1],
                    device_id=peer_at(dy, dx, dz),
                    device_id_type=MESH,
                )
                if dy or dx:
                    copy.start()
                else:
                    pl.when(jnp.logical_not(alone))(copy.start)

    def wait_pair(turn, which):
        pltpu.make_async_copy(pair.at[turn], pair.at[turn], sum_sem.at[which, turn, 0]).wait()

    def wait_far(turn, which):
        got = far.at[turn, pl.ds(0, cols - 1)]
        pltpu.make_async_copy(got, got, sum_sem.at[which, turn, 1]).wait()

    first_col = jnp.where(col == 0, 1.0, 0.0).astype(F32)
    last_col = jnp.where(col == cols - 1, 1.0, 0.0).astype(F32)
    lanes = lax.broadcasted_iota(jnp.int32, (1, 128), 1)
    penalty, rescale, carry_c, carry_s = 1.0, 0.0, 0.0, 0.0

    def scalar(x):
        return x if isinstance(x, float) else x[0, 0]

    for turn in range(ITERS):
        start = turn == 0
        old_c, old_s = carry_c, carry_s
        pc_v = penalty * old_c
        sigma_v = 1.0 - pc_v * old_s
        share_v = 1.0 / (1.0 + penalty)
        carry_s = 1.0 + old_c * old_s
        bound, cut = scalar(WEIGHT_TV / penalty), scalar(WEIGHT_SPARSE / penalty)
        pc, sigma, scale_c = scalar(pc_v), scalar(sigma_v), scalar(old_c)
        share, ratio, scale_s = scalar(share_v), scalar(penalty * share_v), scalar(carry_s)
        factor = scalar(rescale)
        for copy in rim_copies + halo_copies:
            copy.wait()

        def combined(a, b):
            return a if start else a + factor * b

        def place(i, carry):
            value = combined(part_a[rows_of(i), :], part_b[rows_of(i), :])
            est[i, 0:128, :] = value
            return carry

        lax.fori_loop(0, 8, place, 0)
        if start:
            est[8, 0:128, :] = solve(halo[0, 0])
            rims = solve(jnp.concatenate([rim_left[0, 0:8, :], rim_right[0, 0:8, :]], axis=0))
            from_left, from_right = rims[0:8], rims[8:16]
            own_first, own_last = own_rims[0], own_rims[1]
        else:
            est[8, 0:128, :] = combined(halo[turn, 0], halo[turn, 1])
            own_first = combined(rim_send[turn, 0, 0:8, :], rim_send[turn, 0, 8:16, :])
            own_last = combined(rim_send[turn, 1, 0:8, :], rim_send[turn, 1, 8:16, :])
            from_right = combined(rim_right[turn, 0:8, :], rim_right[turn, 8:16, :])
            from_left = combined(rim_left[turn, 0:8, :], rim_left[turn, 8:16, :])
        from_right = jnp.where(last_col > 0.0, own_last, from_right)
        from_left = jnp.where(first_col > 0.0, own_first, from_left)
        for i in range(8):
            est[i, 128:129, :] = from_right[i : i + 1, :]

        g_diff = own_first - from_left
        g_sum = g_diff if start else g_diff + factor * ghost[...]
        g_dual = jnp.clip(g_sum, -bound, bound)
        g_arg = g_diff - (g_sum - g_dual)
        ghost[...] = g_dual
        for i in range(8):
            right_arg[i, 7:8, :] = g_arg[i : i + 1, :]
            right_dual[i, 7:8, :] = g_dual[i : i + 1, :]

        def update(i, off, totals):
            at = pl.ds(off, CHUNK)
            shifted = pl.ds(off + 8, CHUNK)
            flat = pl.ds(pl.multiple_of(i * 128 + off, CHUNK), CHUNK)
            primal, dual, data = totals
            e = est[i, at, :]
            half = e.astype(BF16)
            gh = jnp.dot(jnp.concatenate([half, half], axis=1), gram2[...], preferred_element_type=F32)
            h = half.astype(F32)
            w = proj[flat, :]
            if start:
                data = data + fold(h * (gh - 2.0 * w))
                mix[flat, :] = h
                gram_mix[flat, :] = gh
            else:
                y, gy = mix[flat, :], gram_mix[flat, :]
                data = data + fold((h - pc * y) * (gh - pc * gy - (2.0 * sigma) * w))
                mix[flat, :] = h + scale_c * y
                gram_mix[flat, :] = gh + scale_c * gy
            t = e if start else e + factor * sparse_dual[flat, :]
            fresh = jnp.maximum(t - cut, 0.0)
            gap = e - fresh
            primal = primal + fold(gap * gap)
            move = fresh if start else fresh - sparse_var[flat, :]
            dual = dual + fold(move * move)
            sparse_var[flat, :] = fresh
            sparse_dual[flat, :] = t - fresh
            d = est[i + 1, at, :] - e
            t = d if start else d + factor * down_dual[flat, :]
            clipped = jnp.clip(t, -bound, bound)
            fresh = t - clipped
            gap = d - fresh
            move = fresh if start else fresh - down_var[flat, :]
            weight = jnp.where((i == 7) & (row == 1), 0.0, 1.0).astype(F32)
            primal = primal + weight * fold(gap * gap)
            dual = dual + weight * fold(move * move)
            down_var[flat, :] = fresh
            down_dual[flat, :] = clipped
            down_arg[flat, :] = gap
            d = est[i, pl.ds(off + 1, CHUNK), :] - e
            t = d if start else d + factor * right_dual[i, shifted, :]
            clipped = jnp.clip(t, -bound, bound)
            fresh = t - clipped
            gap = d - fresh
            primal = primal + fold(gap * gap)
            move = fresh if start else fresh - right_var[flat, :]
            dual = dual + fold(move * move)
            right_var[flat, :] = fresh
            right_dual[i, shifted, :] = clipped
            right_arg[i, shifted, :] = gap
            return primal, dual, data

        def update_row(i, totals):
            for off in range(0, 128, CHUNK):
                totals = update(i, off, totals)
            return totals

        zero = jnp.zeros((8, 128), F32)
        primal, dual, data = lax.fori_loop(0, 8, update_row, (zero, zero, zero))
        data = (data + (sigma * sigma) * square) * (share * share)
        line_p = jnp.sum(primal + data, axis=0, keepdims=True)
        line_d = jnp.sum(dual, axis=0, keepdims=True)
        line_p = line_p + pltpu.roll(line_p, 64, 1)
        line_d = line_d + pltpu.roll(line_d, 64, 1)
        line = jnp.where(lanes < 64, line_p, line_d)
        sums[turn, 0] = line
        send_pair(turn)

        final = turn == ITERS - 1

        def rhs(i):
            flat = rows_of(i)
            above = rows_of(jnp.maximum(i - 1, 0))
            has_above = jnp.where(i > 0, 1.0, 0.0).astype(F32)
            w = proj[flat, :]
            we = gram_mix[flat, :] - scale_s * w
            at = pl.ds(8, 128)
            before = pl.ds(7, 128)
            adj_a = (has_above * down_arg[above, :] - down_arg[flat, :]) + (
                right_arg[i, before, :] - right_arg[i, at, :]
            )
            adj_b = (has_above * down_dual[above, :] - down_dual[flat, :]) + (
                right_dual[i, before, :] - right_dual[i, at, :]
            )
            a = w + ratio * we + sparse_var[flat, :] + PROX * est[i, 0:128, :] - adj_a
            b = -(share * we + sparse_dual[flat, :] + adj_b)
            return a, b

        def prepare(i, carry):
            a, b = rhs(i)
            a, b = solve(a), solve(b)
            part_a[rows_of(i), :] = a
            part_b[rows_of(i), :] = b
            put_rims(turn + 1, i, 0, a)
            put_rims(turn + 1, i, 1, b)
            return carry

        def prepare_final(i, carry):
            a, b = rhs(i)
            out_ref[jnp.where(row == 1, 7 - i, i)] = solve_turned(a)
            turned = solve_turned(b)
            part_b[rows_of(i), 0:128] = turned[0:128, :]
            part_b[rows_of(i), 128:256] = turned[128:256, :]
            return carry

        work = prepare_final if final else prepare
        lax.fori_loop(0, 2, work, 0)
        wait_pair(turn, 1)
        line = line + pair[turn]
        sums[turn, 1] = line
        far[turn, pl.ds(col, 1), :] = line

        def send_and_work(n, carry):
            for one in (2 * n, 2 * n + 1):
                away = lax.div(one + 1, 2)
                dz = jnp.where(lax.rem(one, 2) == 1, half - away, half + away)
                send_sums(turn, dz, one == depth - 1)
            return work(n + 2, carry)

        lax.fori_loop(0, half, send_and_work, 0)
        lax.fori_loop(half + 2, 8, work, 0)
        if not final:
            rim_copies = send_rims(turn + 1)
            halo_copies = [send_halo(turn + 1, 0, part_a), send_halo(turn + 1, 1, part_b)]
        wait_far(turn, 1)
        line = jnp.sum(far[turn], axis=0, keepdims=True)
        total_p = jnp.sum(jnp.where(lanes < 64, line, 0.0), axis=1, keepdims=True)
        total_d = jnp.sum(jnp.where(lanes < 64, 0.0, line), axis=1, keepdims=True)
        root = jnp.sqrt(jnp.sqrt((total_p + 1.0) / (penalty * penalty * total_d + 1.0)))
        following = penalty * root
        rescale = penalty / following
        carry_c = rescale * share_v
        penalty = following

    factor = scalar(rescale)

    def finish(i, carry):
        at = jnp.where(row == 1, 7 - i, i)
        out_ref[at, 0:128, :] = out_ref[at, 0:128, :] + factor * part_b[rows_of(i), 0:128]
        out_ref[at, 128:256, :] = out_ref[at, 128:256, :] + factor * part_b[rows_of(i), 128:256]
        return carry

    lax.fori_loop(0, 8, finish, 0)
    for turn in range(ITERS):
        wait_pair(turn, 0)
        wait_far(turn, 0)


def run(sizes, observed, shard):
    ys, xs, depth = sizes
    cols = ys * xs * depth
    channels = 8 * cols
    field = pltpu.VMEM((1024, 256), F32)
    padded = pltpu.VMEM((8, PAD, 256), F32)
    rims = pltpu.VMEM((ITERS, 16, 256), F32)
    return pl.pallas_call(
        functools.partial(kernel, sizes),
        out_shape=jax.ShapeDtypeStruct((8, 256, 128), F32),
        in_specs=[pl.BlockSpec(memory_space=pl.ANY), VMEM],
        out_specs=VMEM,
        scratch_shapes=[
            pltpu.VMEM((channels, 8, 128), BF16),
            pltpu.VMEM((channels * 8, 128), F32),
            pltpu.VMEM((1024, channels), BF16),
            pltpu.VMEM((16, 128), BF16),
            pltpu.VMEM((cols, 16, 128), BF16),
            pltpu.VMEM((channels, 256), BF16),
            pltpu.VMEM((72, 128), F32),
            pltpu.VMEM((256, 256), F32),
            pltpu.VMEM((512, 256), BF16),
            pltpu.VMEM((768, 256), BF16),
            field,
            pltpu.VMEM((2, 8, 256), F32),
            pltpu.VMEM((9, PAD, 256), F32),
            field,
            field,
            pltpu.VMEM((ITERS, 2, 16, 256), F32),
            rims,
            rims,
            pltpu.VMEM((ITERS, 2, 128, 256), F32),
            pltpu.VMEM((8, 256), F32),
            field,
            field,
            field,
            field,
            field,
            field,
            padded,
            padded,
            field,
            field,
            pltpu.VMEM((ITERS, 2, 1, 128), F32),
            pltpu.VMEM((ITERS, 1, 128), F32),
            pltpu.VMEM((ITERS, cols, 128), F32),
            pltpu.SemaphoreType.DMA(()),
            pltpu.SemaphoreType.DMA((6,)),
            pltpu.SemaphoreType.DMA((2, ITERS, 2)),
            pltpu.SemaphoreType.DMA((2, ITERS, 2)),
            pltpu.SemaphoreType.DMA((2, ITERS, 2)),
        ],
        compiler_params=pltpu.CompilerParams(
            collective_id=0, has_side_effects=True, vmem_limit_bytes=48 * 2**20
        ),
        name="unmix",
    )(observed, shard)


def on_device(sizes, observed, library):
    return run(sizes, observed, library).transpose(1, 0, 2)


def solution(mesh):
    sizes = (4, 4, 8) if mesh.shape["col"] == 128 else (2, 2, 2)
    return jax.shard_map(
        functools.partial(on_device, sizes),
        mesh=mesh,
        in_specs=(P(None, "row", "col"), P("col", None)),
        out_specs=P(None, "row", "col"),
        check_vma=False,
    )
```

time: 95.3 us -> 75.8 us (0.80)
  Pallas kernels: 90.9 us -> 71.8 us
    pallas_call x3 -> x1, Pallas kernels: 90.9 us -> 71.8 us  [run(): pl.pallas_call(functools.partial(kernel, sizes), out_shape=jax.ShapeDtype...]
where the time goes in v1:
time: 75.8 us; the launch traced here: 75.7 us
  Pallas kernels  71.8 us (95%)
  local copies, waits for them, and re-layouts  3.86 us (5%)
    pallas_call x1, Pallas kernels, run(): pl.pallas_call(functools.partial(kernel, sizes), out_shape=jax.ShapeDtype...  71.8 us
    unnamed x4, local copies, waits for them, and re-layouts  2.28 us
    transpose x1, local copies, waits for them, and re-layouts, on_device(): return run(sizes, observed, library).transpose(1, 0, 2)  1.58 us

profile of v1, /device:TPU:1, one launch (start us, length us, event | category | flops | bytes accessed | tf_op | source)
XLA Modules:
  0.0 75.7 jit_solution(10149533814608374851)
XLA Ops:
  0.0 0.0 copy-start
  0.0 1.6 %copy-done = bf16[1024,8,128]{2,1,0:T(8,128)(2,1)S(1)} copy-done((bf16[1024,8,128]{2,1,0:T(8,128)(2,1)S(1)}, bf16[1024,8,128]{2,1,0:T(8,128)(2,1)}, u32[]{:S(2)}) %copy-start) | copy-done | bytes 2097176
  1.6 0.0 copy-start.1
  1.6 0.7 copy-done.1
  2.3 71.8 %unmix.1 = f32[8,256,128]{2,1,0:T(8,128)S(1)} custom-call(bf16[1024,8,128]{2,1,0:T(8,128)(2,1)S(1)} %copy-done, bf16[8,256]{1,0:T(8,128)(2,1)S(1)} %copy-done.1), custom_call_target="tpu_custom_call" | custom-call | tf_op jit(solution)/shard_map/unmix/pallas_call | solution.py:620
  74.1 1.6 %copy.3 = f32[256,8,128]{2,1,0:T(8,128)} copy(f32[256,8,128]{2,0,1:T(8,128)S(1)} %bitcast.1) | data formatting | bytes 2097152 | tf_op jit(solution)/shard_map/transpose | solution.py:673
Async XLA Ops:
  0.0 1.6 %copy-start = (bf16[1024,8,128]{2,1,0:T(8,128)(2,1)S(1)}, bf16[1024,8,128]{2,1,0:T(8,128)(2,1)}, u32[]{:S(2)}) copy-start(bf16[1024,8,128]{2,1,0:T(8,128)(2,1)} %obs_ref.1) | copy-start | bytes 6291460
  1.6 0.7 copy-start.1

commit v2 on v1

--- a/solution.py
+++ b/solution.py
@@ -128,6 +128,7 @@
     shard_ref,
     out_ref,
     obs,
+    own_shard,
     wide,
     turned_obs,
     packed,
@@ -161,7 +162,9 @@
     pair,
     far,
     obs_sem,
+    shard_sem,
     gather_sem,
+    plane_sem,
     halo_sem,
     rim_sem,
     sum_sem,
@@ -190,14 +193,14 @@
 
     obs_copy = pltpu.make_async_copy(obs_ref, obs, obs_sem)
     obs_copy.start()
+    shard_copy = pltpu.make_async_copy(shard_ref, own_shard, shard_sem)
+    shard_copy.start()
     barrier = pltpu.get_barrier_semaphore()
-    for dz in range(depth):
-        for dy in range(ys):
-            for dx in range(xs):
-                if dy or dx or dz:
-                    pl.semaphore_signal(barrier, inc=1, device_id=peer_at(dy, dx, dz), device_id_type=MESH)
-    pl.semaphore_signal(barrier, inc=1, device_id=core_peer, device_id_type=MESH)
-    shard = shard_ref[...].astype(F32)
+    peers = [z_peer(n) for n in range(1, depth)] + [plane_peer(n) for n in range(1, planes)] + [core_peer]
+    for peer in peers:
+        pl.semaphore_signal(barrier, inc=1, device_id=peer, device_id_type=MESH)
+    shard_copy.wait()
+    shard = own_shard[...].astype(F32)
     packed[...] = jnp.concatenate([shard[:, :128], shard[:, 128:]], axis=0).astype(BF16)
     mine = parity * (cols // 2) + plane * half + lax.div(z, 2)
     obs_copy.wait()
@@ -209,7 +212,7 @@
         return total + jnp.sum(part * part, axis=0)
 
     square = lax.fori_loop(0, channels // 16, widen, jnp.zeros((8, 128), F32))
-    pl.semaphore_wait(barrier, cols)
+    pl.semaphore_wait(barrier, len(peers))
 
     @pl.when(row == parity)
     def _():
@@ -243,37 +246,48 @@
         got = shards.at[pl.ds(0, half)]
         pltpu.make_async_copy(got, got, gather_sem.at[1]).wait()
 
-    block = shards.at[pl.ds(row * (cols // 2) + plane * half, half)]
+    def block_of(dy, dx):
+        other = lax.rem(y + ys - dy, ys) * xs + lax.rem(x + xs - dx, xs)
+        return shards.at[pl.ds(row * (cols // 2) + other * half, half)]
+
+    def pass_over(block):
+        pltpu.make_async_remote_copy(
+            src_ref=block,
+            dst_ref=block,
+            send_sem=gather_sem.at[3],
+            recv_sem=gather_sem.at[4],
+            device_id=core_peer,
+            device_id_type=MESH,
+        ).start()
+
+    block = block_of(0, 0)
     for step in range(1, planes):
         pltpu.make_async_remote_copy(
             src_ref=block,
             dst_ref=block,
             send_sem=gather_sem.at[2],
-            recv_sem=gather_sem.at[3],
+            recv_sem=plane_sem.at[step],
             device_id=plane_peer(step),
             device_id_type=MESH,
         ).start()
+    pass_over(block)
     lax.fori_loop(4, 8, turn_rows, 0)
-    got = shards.at[pl.ds(0, half * (planes - 1))]
-    pltpu.make_async_copy(got, got, gather_sem.at[3]).wait()
-    own_half = shards.at[pl.ds(row * (cols // 2), cols // 2)]
-    swap = pltpu.make_async_remote_copy(
-        src_ref=own_half,
-        dst_ref=own_half,
-        send_sem=gather_sem.at[4],
-        recv_sem=gather_sem.at[5],
-        device_id=core_peer,
-        device_id_type=MESH,
-    )
-    swap.start()
+    nearest = sorted(range(1, planes), key=lambda n: min(n // xs, ys - n // xs) + min(n % xs, xs - n % xs))
+    for step in nearest:
+        got = block_of(step // xs, step % xs)
+        pltpu.make_async_copy(got, got, plane_sem.at[step]).wait()
+        pass_over(got)
+    other_half = shards.at[pl.ds((1 - row) * (cols // 2), cols // 2)]
+    pltpu.make_async_copy(other_half, other_half, gather_sem.at[4]).wait()
 
     @pl.when(row == parity)
     def _():
         sent = shards.at[pl.ds(0, depth - 1)]
         pltpu.make_async_copy(sent, sent, gather_sem.at[0]).wait()
 
-    pltpu.make_async_copy(got, got, gather_sem.at[2]).wait()
-    swap.wait()
+    sent = shards.at[pl.ds(0, half * (planes - 1))]
+    pltpu.make_async_copy(sent, sent, gather_sem.at[2]).wait()
+    pltpu.make_async_copy(other_half, other_half, gather_sem.at[3]).wait()
 
     for two in range(cols // 2):
         one = shards[slot_of(2 * two, depth, cols)].astype(F32)
@@ -283,12 +297,6 @@
 
     def rows_of(x):
         return pl.ds(pl.multiple_of(x * 128, 128), 128)
-
-    for i in range(8):
-        value = jnp.dot(turned_obs[128 * i : 128 * i + 128, :], lib[...], preferred_element_type=F32)
-        proj[128 * i : 128 * i + 128, :] = value
-        rim_send[0, 0, i : i + 1, :] = value[0:1, :]
-        rim_send[0, 1, i : i + 1, :] = value[127:128, :]
 
     def send_halo(turn, slot, field):
         copy = pltpu.make_async_remote_copy(
@@ -324,9 +332,6 @@
         to_right.start()
         return [to_left, to_right]
 
-    rim_copies = send_rims(0)
-    halo_copies = [send_halo(0, 0, proj)]
-
     library = lib[...]
     gram = lax.dot_general(library, library, (((0,), (0,)), ((), ())), preferred_element_type=F32)
     high, low = split2(gram)
@@ -334,7 +339,15 @@
     gram2[256:512, :] = low
     same = lax.broadcasted_iota(jnp.int32, (256, 256), 0) == lax.broadcasted_iota(jnp.int32, (256, 256), 1)
     system = gram + jnp.where(same, 1.0 + PROX, 0.0)
+    for i in range(8):
+        value = jnp.dot(turned_obs[128 * i : 128 * i + 128, :], lib[...], preferred_element_type=F32)
+        proj[128 * i : 128 * i + 128, :] = value
+        rim_send[0, 0, i : i + 1, :] = value[0:1, :]
+        rim_send[0, 1, i : i + 1, :] = value[127:128, :]
+
     first_inverse = eliminate(system[:128, :128], work_rows)
+    rim_copies = send_rims(0)
+    halo_copies = [send_halo(0, 0, proj)]
     lead = exact_dot(first_inverse, system[:128, 128:], ((1,), (0,)))
     last_inverse = eliminate(
         system[128:, 128:] - exact_dot(system[128:, :128], lead, ((1,), (0,))), work_rows
@@ -574,15 +587,13 @@
         sums[turn, 1] = line
         far[turn, pl.ds(col, 1), :] = line
 
-        def send_and_work(n, carry):
-            for one in (2 * n, 2 * n + 1):
-                away = lax.div(one + 1, 2)
-                dz = jnp.where(lax.rem(one, 2) == 1, half - away, half + away)
-                send_sums(turn, dz, one == depth - 1)
-            return work(n + 2, carry)
-
-        lax.fori_loop(0, half, send_and_work, 0)
-        lax.fori_loop(half + 2, 8, work, 0)
+        def send_all(n, carry):
+            away = lax.div(n + 1, 2)
+            send_sums(turn, jnp.where(lax.rem(n, 2) == 1, half - away, half + away), n == depth - 1)
+            return carry
+
+        lax.fori_loop(0, depth, send_all, 0)
+        lax.fori_loop(2, 8, work, 0)
         if not final:
             rim_copies = send_rims(turn + 1)
             halo_copies = [send_halo(turn + 1, 0, part_a), send_halo(turn + 1, 1, part_b)]
@@ -613,6 +624,7 @@
 def run(sizes, observed, shard):
     ys, xs, depth = sizes
     cols = ys * xs * depth
+    planes = ys * xs
     channels = 8 * cols
     field = pltpu.VMEM((1024, 256), F32)
     padded = pltpu.VMEM((8, PAD, 256), F32)
@@ -620,10 +632,11 @@
     return pl.pallas_call(
         functools.partial(kernel, sizes),
         out_shape=jax.ShapeDtypeStruct((8, 256, 128), F32),
-        in_specs=[pl.BlockSpec(memory_space=pl.ANY), VMEM],
+        in_specs=[pl.BlockSpec(memory_space=pl.ANY)] * 2,
         out_specs=VMEM,
         scratch_shapes=[
             pltpu.VMEM((channels, 8, 128), BF16),
+            pltpu.VMEM((8, 256), BF16),
             pltpu.VMEM((channels * 8, 128), F32),
             pltpu.VMEM((1024, channels), BF16),
             pltpu.VMEM((16, 128), BF16),
@@ -657,13 +670,15 @@
             pltpu.VMEM((ITERS, 1, 128), F32),
             pltpu.VMEM((ITERS, cols, 128), F32),
             pltpu.SemaphoreType.DMA(()),
-            pltpu.SemaphoreType.DMA((6,)),
+            pltpu.SemaphoreType.DMA(()),
+            pltpu.SemaphoreType.DMA((5,)),
+            pltpu.SemaphoreType.DMA((planes,)),
             pltpu.SemaphoreType.DMA((2, ITERS, 2)),
             pltpu.SemaphoreType.DMA((2, ITERS, 2)),
             pltpu.SemaphoreType.DMA((2, ITERS, 2)),
         ],
         compiler_params=pltpu.CompilerParams(
-            collective_id=0, has_side_effects=True, vmem_limit_bytes=48 * 2**20
+            collective_id=0, has_side_effects=True, vmem_limit_bytes=125 * 2**19
         ),
         name="unmix",
     )(observed, shard)

time: 75.8 us -> 71.2 us (0.939)
  Pallas kernels: 71.8 us -> 68.3 us
  local copies, waits for them, and re-layouts: 3.86 us -> 2.81 us
    pallas_call x1, Pallas kernels: 71.8 us -> 68.3 us  [run(): pl.pallas_call(functools.partial(kernel, sizes), out_shape=jax.ShapeDtype...]
    unnamed x4 -> x0, local copies, waits for them, and re-layouts: 2.28 us -> none
    transpose x1, local copies, waits for them, and re-layouts: 1.58 us -> 2.81 us  [on_device(): return run(sizes, observed, library).transpose(1, 0, 2)]
where the time goes in v2:
time: 71.2 us; the launch traced here: 71.1 us
  Pallas kernels  68.3 us (96%)
  local copies, waits for them, and re-layouts  2.81 us (4%)
    pallas_call x1, Pallas kernels, run(): pl.pallas_call(functools.partial(kernel, sizes), out_shape=jax.ShapeDtype...  68.3 us
    transpose x1, local copies, waits for them, and re-layouts, on_device(): return run(sizes, observed, library).transpose(1, 0, 2)  2.81 us

profile of v2, /device:TPU:1, one launch (start us, length us, event | category | flops | bytes accessed | tf_op | source)
XLA Modules:
  0.0 71.1 jit_solution(16494874698194727490)
XLA Ops:
  0.0 68.3 %unmix.1 = f32[8,256,128]{2,1,0:T(8,128)} custom-call(bf16[1024,8,128]{2,1,0:T(8,128)(2,1)} %obs_ref.1, bf16[8,256]{1,0:T(8,128)(2,1)} %shard_ref.1), custom_call_target="tpu_custom_call" | custom-call | tf_op jit(solution)/shard_map/unmix/pallas_call | solution.py:632
  68.3 2.8 %copy.3 = f32[256,8,128]{2,1,0:T(8,128)} copy(f32[256,8,128]{2,0,1:T(8,128)} %bitcast.1) | data formatting | bytes 2097152 | tf_op jit(solution)/shard_map/transpose | solution.py:688

commit v3 on v2

--- a/solution.py
+++ b/solution.py
@@ -126,7 +126,9 @@
     sizes,
     obs_ref,
     shard_ref,
-    out_ref,
+    out_a,
+    out_b,
+    out_r,
     obs,
     own_shard,
     wide,
@@ -156,7 +158,6 @@
     right_var,
     right_dual,
     right_arg,
-    mix,
     gram_mix,
     sums,
     pair,
@@ -168,6 +169,7 @@
     halo_sem,
     rim_sem,
     sum_sem,
+    result_sem,
 ):
     ys, xs, depth = sizes
     planes, half = ys * xs, depth // 2
@@ -479,20 +481,19 @@
             at = pl.ds(off, CHUNK)
             shifted = pl.ds(off + 8, CHUNK)
             flat = pl.ds(pl.multiple_of(i * 128 + off, CHUNK), CHUNK)
-            primal, dual, data = totals
+            primal, dual, quad, cross, along = totals
             e = est[i, at, :]
             half = e.astype(BF16)
             gh = jnp.dot(jnp.concatenate([half, half], axis=1), gram2[...], preferred_element_type=F32)
             h = half.astype(F32)
             w = proj[flat, :]
+            quad = quad + fold(h * gh)
+            along = along + fold(h * w)
             if start:
-                data = data + fold(h * (gh - 2.0 * w))
-                mix[flat, :] = h
                 gram_mix[flat, :] = gh
             else:
-                y, gy = mix[flat, :], gram_mix[flat, :]
-                data = data + fold((h - pc * y) * (gh - pc * gy - (2.0 * sigma) * w))
-                mix[flat, :] = h + scale_c * y
+                gy = gram_mix[flat, :]
+                cross = cross + fold(h * gy)
                 gram_mix[flat, :] = gh + scale_c * gy
             t = e if start else e + factor * sparse_dual[flat, :]
             fresh = jnp.maximum(t - cut, 0.0)
@@ -525,7 +526,7 @@
             right_var[flat, :] = fresh
             right_dual[i, shifted, :] = clipped
             right_arg[i, shifted, :] = gap
-            return primal, dual, data
+            return primal, dual, quad, cross, along
 
         def update_row(i, totals):
             for off in range(0, 128, CHUNK):
@@ -533,8 +534,15 @@
             return totals
 
         zero = jnp.zeros((8, 128), F32)
-        primal, dual, data = lax.fori_loop(0, 8, update_row, (zero, zero, zero))
-        data = (data + (sigma * sigma) * square) * (share * share)
+        primal, dual, quad, cross, along = lax.fori_loop(0, 8, update_row, (zero,) * 5)
+        data = quad - 2.0 * along + square
+        if not start:
+            data = (quad - (2.0 * pc) * cross + (pc * pc) * old_quad) - (2.0 * sigma) * (along - pc * old_along)
+            data = data + (sigma * sigma) * square
+            quad = quad + (2.0 * scale_c) * cross + (scale_c * scale_c) * old_quad
+            along = along + scale_c * old_along
+        data = data * (share * share)
+        old_quad, old_along = quad, along
         line_p = jnp.sum(primal + data, axis=0, keepdims=True)
         line_d = jnp.sum(dual, axis=0, keepdims=True)
         line_p = line_p + pltpu.roll(line_p, 64, 1)
@@ -574,10 +582,9 @@
 
         def prepare_final(i, carry):
             a, b = rhs(i)
-            out_ref[jnp.where(row == 1, 7 - i, i)] = solve_turned(a)
-            turned = solve_turned(b)
-            part_b[rows_of(i), 0:128] = turned[0:128, :]
-            part_b[rows_of(i), 128:256] = turned[128:256, :]
+            spot = jnp.where(flip, 7 - i, i)
+            wide[pl.ds(spot, 256, stride=8), :] = solve_turned(a)
+            wide[pl.ds(2048 + spot, 256, stride=8), :] = solve_turned(b)
             return carry
 
         work = prepare_final if final else prepare
@@ -597,6 +604,13 @@
         if not final:
             rim_copies = send_rims(turn + 1)
             halo_copies = [send_halo(turn + 1, 0, part_a), send_halo(turn + 1, 1, part_b)]
+        else:
+            results = [
+                pltpu.make_async_copy(wide.at[pl.ds(2048 * n, 2048)], ref, result_sem.at[n])
+                for n, ref in enumerate((out_a, out_b))
+            ]
+            for copy in results:
+                copy.start()
         wait_far(turn, 1)
         line = jnp.sum(far[turn], axis=0, keepdims=True)
         total_p = jnp.sum(jnp.where(lanes < 64, line, 0.0), axis=1, keepdims=True)
@@ -607,15 +621,9 @@
         carry_c = rescale * share_v
         penalty = following
 
-    factor = scalar(rescale)
-
-    def finish(i, carry):
-        at = jnp.where(row == 1, 7 - i, i)
-        out_ref[at, 0:128, :] = out_ref[at, 0:128, :] + factor * part_b[rows_of(i), 0:128]
-        out_ref[at, 128:256, :] = out_ref[at, 128:256, :] + factor * part_b[rows_of(i), 128:256]
-        return carry
-
-    lax.fori_loop(0, 8, finish, 0)
+    out_r[...] = jnp.broadcast_to(rescale, (8, 128))
+    for copy in results:
+        copy.wait()
     for turn in range(ITERS):
         wait_pair(turn, 0)
         wait_far(turn, 0)
@@ -631,13 +639,17 @@
     rims = pltpu.VMEM((ITERS, 16, 256), F32)
     return pl.pallas_call(
         functools.partial(kernel, sizes),
-        out_shape=jax.ShapeDtypeStruct((8, 256, 128), F32),
+        out_shape=[
+            jax.ShapeDtypeStruct((2048, 128), F32),
+            jax.ShapeDtypeStruct((2048, 128), F32),
+            jax.ShapeDtypeStruct((8, 128), F32),
+        ],
         in_specs=[pl.BlockSpec(memory_space=pl.ANY)] * 2,
-        out_specs=VMEM,
+        out_specs=[pl.BlockSpec(memory_space=pl.ANY)] * 2 + [VMEM],
         scratch_shapes=[
             pltpu.VMEM((channels, 8, 128), BF16),
             pltpu.VMEM((8, 256), BF16),
-            pltpu.VMEM((channels * 8, 128), F32),
+            pltpu.VMEM((max(channels * 8, 4096), 128), F32),
             pltpu.VMEM((1024, channels), BF16),
             pltpu.VMEM((16, 128), BF16),
             pltpu.VMEM((cols, 16, 128), BF16),
@@ -664,7 +676,6 @@
             field,
             padded,
             padded,
-            field,
             field,
             pltpu.VMEM((ITERS, 2, 1, 128), F32),
             pltpu.VMEM((ITERS, 1, 128), F32),
@@ -676,6 +687,7 @@
             pltpu.SemaphoreType.DMA((2, ITERS, 2)),
             pltpu.SemaphoreType.DMA((2, ITERS, 2)),
             pltpu.SemaphoreType.DMA((2, ITERS, 2)),
+            pltpu.SemaphoreType.DMA((2,)),
         ],
         compiler_params=pltpu.CompilerParams(
             collective_id=0, has_side_effects=True, vmem_limit_bytes=125 * 2**19
@@ -685,7 +697,8 @@
 
 
 def on_device(sizes, observed, library):
-    return run(sizes, observed, library).transpose(1, 0, 2)
+    a, b, rescale = run(sizes, observed, library)
+    return (a + rescale[0, 0] * b).reshape(256, 8, 128)
 
 
 def solution(mesh):

time: 71.2 us -> 72.3 us (1.015)
  other arithmetic: 0 us -> 3.23 us
  local copies, waits for them, and re-layouts: 2.81 us -> 1.19 us
    reshape x0 -> x1, other arithmetic: none -> 3.23 us  [on_device(): return (a + rescale[0, 0] * b).reshape(256, 8, 128)]
    transpose x1 -> x0, local copies, waits for them, and re-layouts: 2.81 us -> none  [on_device(): return run(sizes, observed, library).transpose(1, 0, 2)]
    slice x0 -> x1, local copies, waits for them, and re-layouts: none -> 1.19 us  [on_device(): return (a + rescale[0, 0] * b).reshape(256, 8, 128)]
where the time goes in v3:
time: 72.3 us; the launch traced here: 72.2 us
  Pallas kernels  67.7 us (94%)
  other arithmetic  3.23 us (4%)
  local copies, waits for them, and re-layouts  1.19 us (2%)
    pallas_call x1, Pallas kernels, run(): pl.pallas_call(functools.partial(kernel, sizes), out_shape=[jax.ShapeDtyp...  67.7 us
    reshape x1, other arithmetic, on_device(): return (a + rescale[0, 0] * b).reshape(256, 8, 128)  3.23 us

profile of v3, /device:TPU:1, one launch (start us, length us, event | category | flops | bytes accessed | tf_op | source)
XLA Modules:
  0.0 72.2 jit_solution(4660197917388367963)
XLA Ops:
  0.0 67.7 %unmix.1 = (f32[2048,128]{1,0:T(8,128)}, f32[2048,128]{1,0:T(8,128)}, f32[8,128]{1,0:T(8,128)}) custom-call(bf16[1024,8,128]{2,1,0:T(8,128)(2,1)} %obs_ref.1, bf16[8,256]{1,0:T(8,128)(2,1)} %shard_ref.1), custom_call_target="tpu_custom_call" | custom-call | tf_op jit(solution)/shard_map/unmix/pallas_call | solution.py:640
  67.7 1.2 %slice.3 = f32[1,1]{1,0:T(1,128)} slice(f32[8,128]{1,0:T(8,128)} %get-tuple-element.9), slice={[0:1], [0:1]} | slice | bytes 8 | tf_op jit(solution)/shard_map/slice | solution.py:701
  68.9 3.2 %add_bitcast_fusion = f32[256,8,128]{2,1,0:T(8,128)} fusion(f32[2048,128]{1,0:T(8,128)} %get-tuple-element.8, f32[2048,128]{1,0:T(8,128)} %get-tuple-element.10, f32[]{:T(128)} %bitcast), kind=kLoop, calls=%fused_computation | loop fusion | flops 524288 | bytes 3145732 | tf_op jit(solution)/shard_map/reshape | solution.py:701

commit v4 on v3

--- a/solution.py
+++ b/solution.py
@@ -126,9 +126,7 @@
     sizes,
     obs_ref,
     shard_ref,
-    out_a,
-    out_b,
-    out_r,
+    out_ref,
     obs,
     own_shard,
     wide,
@@ -169,7 +167,6 @@
     halo_sem,
     rim_sem,
     sum_sem,
-    result_sem,
 ):
     ys, xs, depth = sizes
     planes, half = ys * xs, depth // 2
@@ -583,8 +580,8 @@
         def prepare_final(i, carry):
             a, b = rhs(i)
             spot = jnp.where(flip, 7 - i, i)
-            wide[pl.ds(spot, 256, stride=8), :] = solve_turned(a)
-            wide[pl.ds(2048 + spot, 256, stride=8), :] = solve_turned(b)
+            out_ref[pl.ds(spot, 256, stride=8), :] = solve_turned(a)
+            wide[pl.ds(spot, 256, stride=8), :] = solve_turned(b)
             return carry
 
         work = prepare_final if final else prepare
@@ -604,13 +601,6 @@
         if not final:
             rim_copies = send_rims(turn + 1)
             halo_copies = [send_halo(turn + 1, 0, part_a), send_halo(turn + 1, 1, part_b)]
-        else:
-            results = [
-                pltpu.make_async_copy(wide.at[pl.ds(2048 * n, 2048)], ref, result_sem.at[n])
-                for n, ref in enumerate((out_a, out_b))
-            ]
-            for copy in results:
-                copy.start()
         wait_far(turn, 1)
         line = jnp.sum(far[turn], axis=0, keepdims=True)
         total_p = jnp.sum(jnp.where(lanes < 64, line, 0.0), axis=1, keepdims=True)
@@ -621,9 +611,14 @@
         carry_c = rescale * share_v
         penalty = following
 
-    out_r[...] = jnp.broadcast_to(rescale, (8, 128))
-    for copy in results:
-        copy.wait()
+    factor = scalar(rescale)
+
+    def finish(i, carry):
+        at = pl.ds(pl.multiple_of(i * 256, 256), 256)
+        out_ref[at, :] = out_ref[at, :] + factor * wide[at, :]
+        return carry
+
+    lax.fori_loop(0, 8, finish, 0)
     for turn in range(ITERS):
         wait_pair(turn, 0)
         wait_far(turn, 0)
@@ -639,17 +634,13 @@
     rims = pltpu.VMEM((ITERS, 16, 256), F32)
     return pl.pallas_call(
         functools.partial(kernel, sizes),
-        out_shape=[
-            jax.ShapeDtypeStruct((2048, 128), F32),
-            jax.ShapeDtypeStruct((2048, 128), F32),
-            jax.ShapeDtypeStruct((8, 128), F32),
-        ],
-        in_specs=[pl.BlockSpec(memory_space=pl.ANY)] * 2,
-        out_specs=[pl.BlockSpec(memory_space=pl.ANY)] * 2 + [VMEM],
+        out_shape=jax.ShapeDtypeStruct((2048, 128), F32),
+        in_specs=[pl.BlockSpec(memory_space=pltpu.HBM)] * 2,
+        out_specs=VMEM,
         scratch_shapes=[
             pltpu.VMEM((channels, 8, 128), BF16),
             pltpu.VMEM((8, 256), BF16),
-            pltpu.VMEM((max(channels * 8, 4096), 128), F32),
+            pltpu.VMEM((max(channels * 8, 2048), 128), F32),
             pltpu.VMEM((1024, channels), BF16),
             pltpu.VMEM((16, 128), BF16),
             pltpu.VMEM((cols, 16, 128), BF16),
@@ -687,18 +678,16 @@
             pltpu.SemaphoreType.DMA((2, ITERS, 2)),
             pltpu.SemaphoreType.DMA((2, ITERS, 2)),
             pltpu.SemaphoreType.DMA((2, ITERS, 2)),
-            pltpu.SemaphoreType.DMA((2,)),
         ],
         compiler_params=pltpu.CompilerParams(
-            collective_id=0, has_side_effects=True, vmem_limit_bytes=125 * 2**19
+            collective_id=0, has_side_effects=True, vmem_limit_bytes=52 * 2**20
         ),
         name="unmix",
     )(observed, shard)
 
 
 def on_device(sizes, observed, library):
-    a, b, rescale = run(sizes, observed, library)
-    return (a + rescale[0, 0] * b).reshape(256, 8, 128)
+    return run(sizes, observed, library).reshape(256, 8, 128)
 
 
 def solution(mesh):

time: 72.3 us -> 68.9 us (0.953)
  other arithmetic: 3.23 us -> 0 us
    reshape x1 -> x0, other arithmetic: 3.23 us -> none  [on_device(): return (a + rescale[0, 0] * b).reshape(256, 8, 128)]
    unnamed x0 -> x3, local copies, waits for them, and re-layouts: none -> 1.66 us
    slice x1 -> x0, local copies, waits for them, and re-layouts: 1.19 us -> none  [on_device(): return (a + rescale[0, 0] * b).reshape(256, 8, 128)]
where the time goes in v4:
time: 68.9 us; the launch traced here: 68.8 us
  Pallas kernels  67.1 us (97%)
  local copies, waits for them, and re-layouts  1.66 us (2%)
    pallas_call x1, Pallas kernels, run(): pl.pallas_call(functools.partial(kernel, sizes), out_shape=jax.ShapeDtype...  67.1 us
    unnamed x3, local copies, waits for them, and re-layouts  1.66 us

profile of v4, /device:TPU:1, one launch (start us, length us, event | category | flops | bytes accessed | tf_op | source)
XLA Modules:
  0.0 68.8 jit_solution(5321221808742417612)
XLA Ops:
  0.0 0.0 copy-start
  0.0 0.7 copy-done
  0.7 67.1 %unmix.1 = f32[2048,128]{1,0:T(8,128)S(1)} custom-call(bf16[1024,8,128]{2,1,0:T(8,128)(2,1)} %obs_ref.1, bf16[8,256]{1,0:T(8,128)(2,1)S(1)} %copy-done), custom_call_target="tpu_custom_call" | custom-call | tf_op jit(solution)/shard_map/unmix/pallas_call | solution.py:635
  67.8 1.0 %copy.4 = f32[256,8,128]{2,1,0:T(8,128)} copy(f32[256,8,128]{2,1,0:T(8,128)S(1)} %bitcast.1) | data formatting | bytes 2097152
Async XLA Ops:
  0.0 0.7 copy-start

commit v5 on v4

--- a/solution.py
+++ b/solution.py
@@ -120,6 +120,24 @@
             part = x[8 * k : 8 * k + 8, 128 * half : 128 * half + 128]
             total = part if total is None else total + part
     return total
+
+
+def walk_of(sizes):
+    ys, xs, depth = sizes
+    limit = ys // 2 + xs // 2 + depth // 2 - 2
+
+    def hops(dy, dx):
+        return min(dy, ys - dy) + min(dx, xs - dx)
+
+    plane = sorted(((dy, dx) for dy in range(ys) for dx in range(xs)), key=lambda o: -hops(*o))
+    walk, extra = [], 0
+    for away in range(depth // 2, -1, -1):
+        signs = 1 if away in (0, depth // 2) else 2
+        far = [o for o in plane if hops(*o) + away >= limit]
+        near = [o for o in plane if hops(*o) + away < limit and (away or o != (0, 0))]
+        walk.append((signs, away, near, far, extra))
+        extra += signs * len(far)
+    return walk, extra
 
 
 def kernel(
@@ -178,6 +196,7 @@
     parity = lax.rem(z, 2)
     flip = row == 1
     core_peer = (1 - row, col)
+    walk, extra = walk_of(sizes)
     left = (row, lax.rem(col + cols - 1, cols))
     right = (row, lax.rem(col + 1, cols))
 
@@ -202,15 +221,6 @@
     shard = own_shard[...].astype(F32)
     packed[...] = jnp.concatenate([shard[:, :128], shard[:, 128:]], axis=0).astype(BF16)
     mine = parity * (cols // 2) + plane * half + lax.div(z, 2)
-    obs_copy.wait()
-
-    def widen(k, total):
-        base = pl.multiple_of(k * 16, 16)
-        part = obs[pl.ds(base, 16)].astype(F32)
-        wide[pl.ds(pl.multiple_of(base * 8, 128), 128), :] = part.reshape(128, 128)
-        return total + jnp.sum(part * part, axis=0)
-
-    square = lax.fori_loop(0, channels // 16, widen, jnp.zeros((8, 128), F32))
     pl.semaphore_wait(barrier, len(peers))
 
     @pl.when(row == parity)
@@ -226,13 +236,22 @@
             ).start()
         shards[mine] = packed[...]
 
+    obs_copy.wait()
+
+    def widen(k, total):
+        base = pl.multiple_of(k * 16, 16)
+        part = obs[pl.ds(base, 16)].astype(F32)
+        wide[pl.ds(pl.multiple_of(base * 8, 128), 128), :] = part.reshape(128, 128)
+        return total + jnp.sum(part * part, axis=0)
+
+    square = lax.fori_loop(0, channels // 16, widen, jnp.zeros((8, 128), F32))
     def turn_rows(i, carry):
         source = jnp.where(flip, 7 - i, i)
         part = wide[pl.ds(source, channels, stride=8), :]
         turned_obs[pl.ds(pl.multiple_of(i * 128, 128), 128), :] = part.T.astype(BF16)
         return carry
 
-    lax.fori_loop(0, 4, turn_rows, 0)
+    lax.fori_loop(0, 3, turn_rows, 0)
 
     @pl.when(row == parity)
     def _():
@@ -270,7 +289,7 @@
             device_id_type=MESH,
         ).start()
     pass_over(block)
-    lax.fori_loop(4, 8, turn_rows, 0)
+    lax.fori_loop(3, 8, turn_rows, 0)
     nearest = sorted(range(1, planes), key=lambda n: min(n // xs, ys - n // xs) + min(n % xs, xs - n % xs))
     for step in nearest:
         got = block_of(step // xs, step % xs)
@@ -395,27 +414,45 @@
             device_id_type=MESH,
         ).start()
 
-    def send_sums(turn, dz, alone):
-        for dy in range(ys):
-            for dx in range(xs):
-                copy = pltpu.make_async_remote_copy(
-                    src_ref=sums.at[turn, 1],
-                    dst_ref=far.at[turn, pl.ds(col, 1)],
-                    send_sem=sum_sem.at[0, turn, 1],
-                    recv_sem=sum_sem.at[1, turn, 1],
-                    device_id=peer_at(dy, dx, dz),
-                    device_id_type=MESH,
-                )
-                if dy or dx:
-                    copy.start()
-                else:
-                    pl.when(jnp.logical_not(alone))(copy.start)
+    def send_line(turn, stage, slot, device):
+        pltpu.make_async_remote_copy(
+            src_ref=sums.at[turn, stage],
+            dst_ref=far.at[turn, pl.ds(slot, 1)],
+            send_sem=sum_sem.at[0, turn, 1],
+            recv_sem=sum_sem.at[1, turn, 1],
+            device_id=device,
+            device_id_type=MESH,
+        ).start()
+
+    def send_far(turn):
+        for signs, away, _, flat, base in walk:
+            def one_sign(sign, carry):
+                dz = sign * (depth - 2 * away) + away
+                for n, (dy, dx) in enumerate(flat):
+                    other, there = peer_at(dy, dx, dz)
+                    send_line(turn, 0, col, (other, there))
+                    send_line(turn, 0, cols + base + sign * len(flat) + n, (1 - other, there))
+                return carry
+
+            if flat:
+                lax.fori_loop(0, signs, one_sign, 0)
+
+    def send_near(turn):
+        for signs, away, flat, _, _ in walk:
+            def one_sign(sign, carry):
+                dz = sign * (depth - 2 * away) + away
+                for dy, dx in flat:
+                    send_line(turn, 1, col, peer_at(dy, dx, dz))
+                return carry
+
+            if flat:
+                lax.fori_loop(0, signs, one_sign, 0)
 
     def wait_pair(turn, which):
         pltpu.make_async_copy(pair.at[turn], pair.at[turn], sum_sem.at[which, turn, 0]).wait()
 
     def wait_far(turn, which):
-        got = far.at[turn, pl.ds(0, cols - 1)]
+        got = far.at[turn, pl.ds(0, cols - 1 + extra)]
         pltpu.make_async_copy(got, got, sum_sem.at[which, turn, 1]).wait()
 
     first_col = jnp.where(col == 0, 1.0, 0.0).astype(F32)
@@ -585,24 +622,19 @@
             return carry
 
         work = prepare_final if final else prepare
-        lax.fori_loop(0, 2, work, 0)
+        send_far(turn)
         wait_pair(turn, 1)
         line = line + pair[turn]
         sums[turn, 1] = line
         far[turn, pl.ds(col, 1), :] = line
-
-        def send_all(n, carry):
-            away = lax.div(n + 1, 2)
-            send_sums(turn, jnp.where(lax.rem(n, 2) == 1, half - away, half + away), n == depth - 1)
-            return carry
-
-        lax.fori_loop(0, depth, send_all, 0)
-        lax.fori_loop(2, 8, work, 0)
+        send_near(turn)
+        lax.fori_loop(0, 8, work, 0)
         if not final:
             rim_copies = send_rims(turn + 1)
             halo_copies = [send_halo(turn + 1, 0, part_a), send_halo(turn + 1, 1, part_b)]
         wait_far(turn, 1)
-        line = jnp.sum(far[turn], axis=0, keepdims=True)
+        line = jnp.sum(far[turn, 0:cols, :], axis=0, keepdims=True)
+        line = line + jnp.sum(far[turn, cols : cols + extra, :], axis=0, keepdims=True)
         total_p = jnp.sum(jnp.where(lanes < 64, line, 0.0), axis=1, keepdims=True)
         total_d = jnp.sum(jnp.where(lanes < 64, 0.0, line), axis=1, keepdims=True)
         root = jnp.sqrt(jnp.sqrt((total_p + 1.0) / (penalty * penalty * total_d + 1.0)))
@@ -628,6 +660,7 @@
     ys, xs, depth = sizes
     cols = ys * xs * depth
     planes = ys * xs
+    extra = walk_of(sizes)[1]
     channels = 8 * cols
     field = pltpu.VMEM((1024, 256), F32)
     padded = pltpu.VMEM((8, PAD, 256), F32)
@@ -670,7 +703,7 @@
             field,
             pltpu.VMEM((ITERS, 2, 1, 128), F32),
             pltpu.VMEM((ITERS, 1, 128), F32),
-            pltpu.VMEM((ITERS, cols, 128), F32),
+            pltpu.VMEM((ITERS, cols + 8 * pl.cdiv(extra, 8), 128), F32),
             pltpu.SemaphoreType.DMA(()),
             pltpu.SemaphoreType.DMA(()),
             pltpu.SemaphoreType.DMA((5,)),

time: 68.9 us -> 68.7 us (level)
  no operation moved by 1% of the time
where the time goes in v5:
time: 68.7 us; the launch traced here: 68.6 us
  Pallas kernels  66.9 us (97%)
  local copies, waits for them, and re-layouts  1.66 us (2%)
    pallas_call x1, Pallas kernels, run(): pl.pallas_call(functools.partial(kernel, sizes), out_shape=jax.ShapeDtype...  66.9 us
    unnamed x3, local copies, waits for them, and re-layouts  1.66 us

profile of v5, /device:TPU:1, one launch (start us, length us, event | category | flops | bytes accessed | tf_op | source)
XLA Modules:
  0.0 68.6 jit_solution(960833301174340568)
XLA Ops:
  0.0 0.0 copy-start
  0.0 0.7 copy-done
  0.7 66.9 %unmix.1 = f32[2048,128]{1,0:T(8,128)S(1)} custom-call(bf16[1024,8,128]{2,1,0:T(8,128)(2,1)} %obs_ref.1, bf16[8,256]{1,0:T(8,128)(2,1)S(1)} %copy-done), custom_call_target="tpu_custom_call" | custom-call | tf_op jit(solution)/shard_map/unmix/pallas_call | solution.py:668
  67.6 1.0 %copy.4 = f32[256,8,128]{2,1,0:T(8,128)} copy(f32[256,8,128]{2,1,0:T(8,128)S(1)} %bitcast.1) | data formatting | bytes 2097152
Async XLA Ops:
  0.0 0.7 %copy-start = (bf16[8,256]{1,0:T(8,128)(2,1)S(1)}, bf16[8,256]{1,0:T(8,128)(2,1)}, u32[]{:S(2)}) copy-start(bf16[8,256]{1,0:T(8,128)(2,1)} %shard_ref.1) | copy-start | bytes 12292

commit v6 on v5

--- a/solution.py
+++ b/solution.py
@@ -394,10 +394,6 @@
         total = total + lax.dot_general(inv3[256:512, :], one, dims, preferred_element_type=F32)
         return total + lax.dot_general(inv3[0:256, :], two, dims, preferred_element_type=F32)
 
-    def put_rims(turn, i, slot, value):
-        rim_send[turn, 0, pl.ds(8 * slot + i, 1), :] = value[0:1, :]
-        rim_send[turn, 1, pl.ds(8 * slot + i, 1), :] = value[127:128, :]
-
     for i in range(8):
         value = solve(proj[128 * i : 128 * i + 128, :])
         part_a[128 * i : 128 * i + 128, :] = value
@@ -605,13 +601,30 @@
             b = -(share * we + sparse_dual[flat, :] + adj_b)
             return a, b
 
-        def prepare(i, carry):
+        def rim_rhs(j):
+            def flat(field):
+                return jnp.concatenate([field[128 * i + j : 128 * i + j + 1, :] for i in range(8)], axis=0)
+
+            def deep(field, k):
+                return jnp.concatenate([field[i, k : k + 1, :] for i in range(8)], axis=0)
+
+            def adjoint(down, side):
+                rows = flat(down)
+                above = jnp.concatenate([jnp.zeros((1, 256), F32), rows[0:7, :]], axis=0)
+                return (above - rows) + (deep(side, 7 + j) - deep(side, 8 + j))
+
+            w = flat(proj)
+            we = flat(gram_mix) - scale_s * w
+            a = w + ratio * we + flat(sparse_var) + PROX * deep(est, j) - adjoint(down_arg, right_arg)
+            b = -(share * we + flat(sparse_dual) + adjoint(down_dual, right_dual))
+            return [a, b]
+
+        def prepare(n, carry):
+            i = 7 - n
             a, b = rhs(i)
             a, b = solve(a), solve(b)
             part_a[rows_of(i), :] = a
             part_b[rows_of(i), :] = b
-            put_rims(turn + 1, i, 0, a)
-            put_rims(turn + 1, i, 1, b)
             return carry
 
         def prepare_final(i, carry):
@@ -627,11 +640,16 @@
         line = line + pair[turn]
         sums[turn, 1] = line
         far[turn, pl.ds(col, 1), :] = line
+        if not final:
+            solved = solve(jnp.concatenate(rim_rhs(0) + rim_rhs(127), axis=0))
+            rim_send[turn + 1, 0] = solved[0:16, :]
+            rim_send[turn + 1, 1] = solved[16:32, :]
+            rim_copies = send_rims(turn + 1)
         send_near(turn)
-        lax.fori_loop(0, 8, work, 0)
+        work(0, 0)
         if not final:
-            rim_copies = send_rims(turn + 1)
             halo_copies = [send_halo(turn + 1, 0, part_a), send_halo(turn + 1, 1, part_b)]
+        lax.fori_loop(1, 8, work, 0)
         wait_far(turn, 1)
         line = jnp.sum(far[turn, 0:cols, :], axis=0, keepdims=True)
         line = line + jnp.sum(far[turn, cols : cols + extra, :], axis=0, keepdims=True)

time: 68.7 us -> 66.4 us (0.967)
  Pallas kernels: 66.9 us -> 64.7 us
    pallas_call x1, Pallas kernels: 66.9 us -> 64.7 us  [run(): pl.pallas_call(functools.partial(kernel, sizes), out_shape=jax.ShapeDtype...]
where the time goes in v6:
time: 66.4 us; the launch traced here: 66.3 us
  Pallas kernels  64.7 us (97%)
  local copies, waits for them, and re-layouts  1.66 us (2%)
    pallas_call x1, Pallas kernels, run(): pl.pallas_call(functools.partial(kernel, sizes), out_shape=jax.ShapeDtype...  64.7 us
    unnamed x3, local copies, waits for them, and re-layouts  1.66 us

profile of v6, /device:TPU:1, one launch (start us, length us, event | category | flops | bytes accessed | tf_op | source)
XLA Modules:
  0.0 66.3 jit_solution(637199243425951077)
XLA Ops:
  0.0 0.0 copy-start
  0.0 0.7 %copy-done = bf16[8,256]{1,0:T(8,128)(2,1)S(1)} copy-done((bf16[8,256]{1,0:T(8,128)(2,1)S(1)}, bf16[8,256]{1,0:T(8,128)(2,1)}, u32[]{:S(2)}) %copy-start) | copy-done | bytes 4120
  0.7 64.7 %unmix.1 = f32[2048,128]{1,0:T(8,128)S(1)} custom-call(bf16[1024,8,128]{2,1,0:T(8,128)(2,1)} %obs_ref.1, bf16[8,256]{1,0:T(8,128)(2,1)S(1)} %copy-done), custom_call_target="tpu_custom_call" | custom-call | tf_op jit(solution)/shard_map/unmix/pallas_call | solution.py:686
  65.4 1.0 %copy.4 = f32[256,8,128]{2,1,0:T(8,128)} copy(f32[256,8,128]{2,1,0:T(8,128)S(1)} %bitcast.1) | data formatting | bytes 2097152
Async XLA Ops:
  0.0 0.7 %copy-start = (bf16[8,256]{1,0:T(8,128)(2,1)S(1)}, bf16[8,256]{1,0:T(8,128)(2,1)}, u32[]{:S(2)}) copy-start(bf16[8,256]{1,0:T(8,128)(2,1)} %shard_ref.1) | copy-start | bytes 12292

commit v7 on v6

--- a/solution.py
+++ b/solution.py
@@ -156,6 +156,7 @@
     inverse,
     gram2,
     inv3,
+    inv_wide,
     proj,
     own_rims,
     est,
@@ -200,8 +201,12 @@
     left = (row, lax.rem(col + cols - 1, cols))
     right = (row, lax.rem(col + 1, cols))
 
+    columns = [
+        [(lax.rem(y + dy, ys) * xs + lax.rem(x + dx, xs)) * depth for dx in range(xs)] for dy in range(ys)
+    ]
+
     def peer_at(dy, dx, dz):
-        return (row, (lax.rem(y + dy, ys) * xs + lax.rem(x + dx, xs)) * depth + lax.rem(z + dz, depth))
+        return (row, columns[dy][dx] + lax.rem(z + dz, depth))
 
     def z_peer(step):
         return peer_at(0, 0, step)
@@ -379,6 +384,9 @@
     inv3[0:256, :] = high
     inv3[256:512, :] = low
     inv3[512:768, :] = high
+    inv_wide[:, 0:256] = high
+    inv_wide[:, 256:512] = low
+    inv_wide[:, 512:768] = high
 
     def stacked(x):
         one, two = split2(x)
@@ -388,11 +396,7 @@
         return jnp.dot(stacked(x), inv3[...], preferred_element_type=F32)
 
     def solve_turned(x):
-        one, two = split2(x)
-        dims = (((1,), (1,)), ((), ()))
-        total = lax.dot_general(inv3[0:256, :], one, dims, preferred_element_type=F32)
-        total = total + lax.dot_general(inv3[256:512, :], one, dims, preferred_element_type=F32)
-        return total + lax.dot_general(inv3[0:256, :], two, dims, preferred_element_type=F32)
+        return lax.dot_general(inv_wide[...], stacked(x), (((1,), (1,)), ((), ())), preferred_element_type=F32)
 
     for i in range(8):
         value = solve(proj[128 * i : 128 * i + 128, :])
@@ -507,15 +511,14 @@
             right_arg[i, 7:8, :] = g_arg[i : i + 1, :]
             right_dual[i, 7:8, :] = g_dual[i : i + 1, :]
 
-        def update(i, off, totals):
+        def update(i, off, half_row, gh_row, totals):
             at = pl.ds(off, CHUNK)
             shifted = pl.ds(off + 8, CHUNK)
             flat = pl.ds(pl.multiple_of(i * 128 + off, CHUNK), CHUNK)
             primal, dual, quad, cross, along = totals
             e = est[i, at, :]
-            half = e.astype(BF16)
-            gh = jnp.dot(jnp.concatenate([half, half], axis=1), gram2[...], preferred_element_type=F32)
-            h = half.astype(F32)
+            gh = gh_row[off : off + CHUNK, :]
+            h = half_row[off : off + CHUNK, :].astype(F32)
             w = proj[flat, :]
             quad = quad + fold(h * gh)
             along = along + fold(h * w)
@@ -559,8 +562,12 @@
             return primal, dual, quad, cross, along
 
         def update_row(i, totals):
+            half_row = est[i, 0:128, :].astype(BF16)
+            gh_row = jnp.dot(
+                jnp.concatenate([half_row, half_row], axis=1), gram2[...], preferred_element_type=F32
+            )
             for off in range(0, 128, CHUNK):
-                totals = update(i, off, totals)
+                totals = update(i, off, half_row, gh_row, totals)
             return totals
 
         zero = jnp.zeros((8, 128), F32)
@@ -622,16 +629,17 @@
         def prepare(n, carry):
             i = 7 - n
             a, b = rhs(i)
-            a, b = solve(a), solve(b)
-            part_a[rows_of(i), :] = a
-            part_b[rows_of(i), :] = b
+            both = solve(jnp.concatenate([a, b], axis=0))
+            part_a[rows_of(i), :] = both[0:128, :]
+            part_b[rows_of(i), :] = both[128:256, :]
             return carry
 
         def prepare_final(i, carry):
             a, b = rhs(i)
             spot = jnp.where(flip, 7 - i, i)
-            out_ref[pl.ds(spot, 256, stride=8), :] = solve_turned(a)
-            wide[pl.ds(spot, 256, stride=8), :] = solve_turned(b)
+            both = solve_turned(jnp.concatenate([a, b], axis=0))
+            out_ref[pl.ds(spot, 256, stride=8), :] = both[:, 0:128]
+            wide[pl.ds(spot, 256, stride=8), :] = both[:, 128:256]
             return carry
 
         work = prepare_final if final else prepare
@@ -700,6 +708,7 @@
             pltpu.VMEM((256, 256), F32),
             pltpu.VMEM((512, 256), BF16),
             pltpu.VMEM((768, 256), BF16),
+            pltpu.VMEM((256, 768), BF16),
             field,
             pltpu.VMEM((2, 8, 256), F32),
             pltpu.VMEM((9, PAD, 256), F32),

time: 66.4 us -> 66.3 us (level)
  no operation moved by 1% of the time
where the time goes in v7:
time: 66.3 us; the launch traced here: 66.2 us
  Pallas kernels  64.6 us (97%)
  local copies, waits for them, and re-layouts  1.66 us (3%)
    pallas_call x1, Pallas kernels, run(): pl.pallas_call(functools.partial(kernel, sizes), out_shape=jax.ShapeDtype...  64.6 us
    unnamed x3, local copies, waits for them, and re-layouts  1.66 us

profile of v7, /device:TPU:1, one launch (start us, length us, event | category | flops | bytes accessed | tf_op | source)
XLA Modules:
  0.0 66.2 jit_solution(1446558982578247485)
XLA Ops:
  0.0 0.0 copy-start
  0.0 0.7 %copy-done = bf16[8,256]{1,0:T(8,128)(2,1)S(1)} copy-done((bf16[8,256]{1,0:T(8,128)(2,1)S(1)}, bf16[8,256]{1,0:T(8,128)(2,1)}, u32[]{:S(2)}) %copy-start) | copy-done | bytes 4120
  0.7 64.6 %unmix.1 = f32[2048,128]{1,0:T(8,128)S(1)} custom-call(bf16[1024,8,128]{2,1,0:T(8,128)(2,1)} %obs_ref.1, bf16[8,256]{1,0:T(8,128)(2,1)S(1)} %copy-done), custom_call_target="tpu_custom_call" | custom-call | tf_op jit(solution)/shard_map/unmix/pallas_call | solution.py:694
  65.3 1.0 %copy.4 = f32[256,8,128]{2,1,0:T(8,128)} copy(f32[256,8,128]{2,1,0:T(8,128)S(1)} %bitcast.1) | data formatting | bytes 2097152
Async XLA Ops:
  0.0 0.7 %copy-start = (bf16[8,256]{1,0:T(8,128)(2,1)S(1)}, bf16[8,256]{1,0:T(8,128)(2,1)}, u32[]{:S(2)}) copy-start(bf16[8,256]{1,0:T(8,128)(2,1)} %shard_ref.1) | copy-start | bytes 12292

commit v8 on v7

--- a/solution.py
+++ b/solution.py
@@ -109,7 +109,7 @@
     return high, (x - high.astype(F32)).astype(BF16)
 
 
-CHUNK = 32
+CHUNK = 16
 PAD = 136
 
 

time: 66.3 us -> 66.5 us (level)
  no operation moved by 1% of the time
where the time goes in v8:
time: 66.5 us; the launch traced here: 66.4 us
  Pallas kernels  64.8 us (97%)
  local copies, waits for them, and re-layouts  1.66 us (2%)
    pallas_call x1, Pallas kernels, run(): pl.pallas_call(functools.partial(kernel, sizes), out_shape=jax.ShapeDtype...  64.8 us
    unnamed x3, local copies, waits for them, and re-layouts  1.66 us

profile of v8, /device:TPU:1, one launch (start us, length us, event | category | flops | bytes accessed | tf_op | source)
XLA Modules:
  0.0 66.4 jit_solution(10156987431184053768)
XLA Ops:
  0.0 0.0 copy-start
  0.0 0.7 %copy-done = bf16[8,256]{1,0:T(8,128)(2,1)S(1)} copy-done((bf16[8,256]{1,0:T(8,128)(2,1)S(1)}, bf16[8,256]{1,0:T(8,128)(2,1)}, u32[]{:S(2)}) %copy-start) | copy-done | bytes 4120
  0.7 64.8 %unmix.1 = f32[2048,128]{1,0:T(8,128)S(1)} custom-call(bf16[1024,8,128]{2,1,0:T(8,128)(2,1)} %obs_ref.1, bf16[8,256]{1,0:T(8,128)(2,1)S(1)} %copy-done), custom_call_target="tpu_custom_call" | custom-call | tf_op jit(solution)/shard_map/unmix/pallas_call | solution.py:694
  65.5 1.0 %copy.4 = f32[256,8,128]{2,1,0:T(8,128)} copy(f32[256,8,128]{2,1,0:T(8,128)S(1)} %bitcast.1) | data formatting | bytes 2097152
Async XLA Ops:
  0.0 0.7 %copy-start = (bf16[8,256]{1,0:T(8,128)(2,1)S(1)}, bf16[8,256]{1,0:T(8,128)(2,1)}, u32[]{:S(2)}) copy-start(bf16[8,256]{1,0:T(8,128)(2,1)} %shard_ref.1) | copy-start | bytes 12292
